TPU v7x, 32 devices: a whole 2x2x4 slice. The times are simulated.
32 devices in a mesh: gx: 4 (over x, core), gy: 4 (over z), gz: 2 (over y).
Axes of the slice: x: 2, y: 2, z: 4, core: 2. Of those that a mesh axis runs over, the one named last changes fastest.
Arguments:
- body_force: float32 [3, 16, 32, 512], P(None, 'gz', 'gx', 'gy'), may hold values from -6 to 6
- viscosity: float32 [16, 32, 512], P('gz', 'gx', 'gy'), may hold values from 0.05 to 0.5
- topography: float32 [256, 4096], P('gx', 'gy'), may hold values from -6 to 6
- kappa: bfloat16 [256, 4096], P('gx', 'gy'), may hold values from 0.019897461 to 0.19921875
Outputs:
- velocity: float32 [3, 16, 32, 512], P(None, 'gz', 'gx', 'gy')
- surface: float32 [256, 4096], P('gx', ('gy', 'gz'))
All inputs are finite; a program needn't handle non-finite values.
Results may differ from a plain program's by a relative error of at most 0.0008.
Values may be sent and summed in bfloat16 or wider, within the bound.
A program may use at most 64 MiB of HBM per device.

v0:
```python
import jax
import jax.numpy as jnp
from jax import lax
from jax.sharding import PartitionSpec as P

ITERS = 2
STEPS = 8


drag = 1.0
time_step = 1.0
load_gain = 4.0


def extended_2(cells, sides, width):
    for axis, dim in sides:
        count = lax.axis_size(axis)
        ends = count - 1
        head = lax.slice_in_dim(cells, 0, width, axis=dim)
        tail = lax.slice_in_dim(cells, cells.shape[dim] - width, cells.shape[dim], axis=dim)
        cells = jnp.concatenate(
            [
                lax.ppermute(tail, axis, [(i, (i + 1) % count) for i in range(ends)]),
                cells,
                lax.ppermute(head, axis, [((i + 1) % count, i) for i in range(ends)]),
            ],
            axis=dim,
        )
    return cells


def spread(block, axis, owner):
    block = jnp.where(lax.axis_index(axis) == owner, block, jnp.zeros_like(block))
    return lax.psum(block, axis)


def shifts():
    found = []
    for depth in (-1, 0, 1):
        for across in (-1, 0, 1):
            for along in (-1, 0, 1):
                if depth != 0 or across != 0 or along != 0:
                    found.append((depth, across, along))
    return found


def window(array, depth, across, along):
    inner_depth = array.shape[-3] - 2
    inner_rows = array.shape[-2] - 2
    inner_cols = array.shape[-1] - 2
    return array[
        ...,
        1 + depth : 1 + depth + inner_depth,
        1 + across : 1 + across + inner_rows,
        1 + along : 1 + along + inner_cols,
    ]


def apply_operator(padded, viscous):
    center = window(padded, 0, 0, 0)
    eta_center = window(viscous, 0, 0, 0)
    total = drag * center
    for depth, across, along in shifts():
        weight = 0.5 / (depth * depth + across * across + along * along)
        coupling = weight * (eta_center + window(viscous, depth, across, along))
        total = total + coupling * (center - window(padded, depth, across, along))
    return total


def cell_rim(field):
    return extended_2(field, (("gx", 2), ("gy", 3), ("gz", 1)), 1)


def flux(slope, conduct):
    return conduct * slope / jnp.sqrt(1.0 + slope * slope)


def diffuse_step(extended, conduct):
    along = flux(extended[:, 1:] - extended[:, :-1], 0.5 * (conduct[:, 1:] + conduct[:, :-1]))
    across = flux(extended[1:, :] - extended[:-1, :], 0.5 * (conduct[1:, :] + conduct[:-1, :]))
    change = along[1:-1, 1:] - along[1:-1, :-1] + across[1:, 1:-1] - across[:-1, 1:-1]
    return extended[1:-1, 1:-1] + time_step * change


def squares(residual):
    return lax.psum(jnp.sum(residual * residual), ("gx", "gy", "gz"))


def local(body_force, viscosity, topography, kappa):
    depth_cells = body_force.shape[1]
    row_cells = body_force.shape[2]
    col_cells = body_force.shape[3]
    rows, cols = topography.shape
    row_ratio = rows // row_cells
    col_ratio = cols // col_cells
    is_top = lax.axis_index("gz") == lax.axis_size("gz") - 1
    load = topography.reshape(row_cells, row_ratio, col_cells, col_ratio).mean(axis=(1, 3))
    force = body_force.at[2, depth_cells - 1].add(jnp.where(is_top, -load_gain * load, 0.0))
    viscous = cell_rim(viscosity[None])
    velocity = jnp.zeros_like(force)
    residual = force
    direction = force
    norm_now = squares(residual)
    for step in range(ITERS):
        image = apply_operator(cell_rim(direction), viscous)
        alpha = norm_now / lax.psum(jnp.sum(direction * image), ("gx", "gy", "gz"))
        velocity = velocity + alpha * direction
        if step + 1 < ITERS:
            residual = residual - alpha * image
            norm_next = squares(residual)
            direction = residual + norm_next / norm_now * direction
            norm_now = norm_next
    top = spread(velocity[2, depth_cells - 1], "gz", lax.axis_size("gz") - 1)
    rise = jnp.broadcast_to(
        top[:, None, :, None], (row_cells, row_ratio, col_cells, col_ratio)
    ).reshape(rows, cols)
    reach = STEPS
    conduct = extended_2(kappa, (("gx", 0), ("gy", 1)), reach).astype(jnp.float32)
    wide_height = extended_2(topography.astype(jnp.bfloat16), (("gx", 0), ("gy", 1)), STEPS).astype(
        topography.dtype
    )
    surf_row_first = lax.axis_index("gx") * rows
    surf_col_first = lax.axis_index("gy") * cols
    total_rows = rows * lax.axis_size("gx")
    total_cols = cols * lax.axis_size("gy")
    for step in range(STEPS):
        margin = STEPS - step - 1
        wide_height = diffuse_step(
            wide_height, conduct[step : conduct.shape[0] - step, step : conduct.shape[1] - step]
        )
        row_index = surf_row_first - margin + jnp.arange(rows + 2 * margin, dtype=jnp.int32)
        col_index = surf_col_first - margin + jnp.arange(cols + 2 * margin, dtype=jnp.int32)
        inside = ((row_index >= 0) & (row_index < total_rows))[:, None] & (
            (col_index >= 0) & (col_index < total_cols)
        )[None, :]
        wide_height = jnp.where(inside, wide_height, 0.0)
    surface = wide_height + STEPS * time_step * rise
    share = cols // lax.axis_size("gz")
    surface = lax.dynamic_slice_in_dim(surface, lax.axis_index("gz") * share, share, 1)
    return (velocity, surface)


def solution(mesh):
    in_specs = (P(None, "gz", "gx", "gy"), P("gz", "gx", "gy"), P("gx", "gy"), P("gx", "gy"))
    out_specs = (P(None, "gz", "gx", "gy"), P("gx", ("gy", "gz")))
    return jax.shard_map(local, mesh=mesh, in_specs=in_specs, out_specs=out_specs, check_vma=False)
```

profile of v0, /device:TPU:0, one launch (start us, length us, event | category | flops | bytes accessed | tf_op | source)
XLA Modules:
  0.0 245.6 jit_solution(16424226946786336233)
XLA Ops:
  0.7 4.6 %reshape.178 = f32[8,8,128,8]{3,2,1,0:T(8,128)} reshape(f32[64,1024]{1,0:T(8,128)} %param.8) | data formatting | bytes 524288 | tf_op jit(solution)/shard_map/reshape | solution.py:97
  5.2 2.5 %reduce_sum.45 = f32[8,128]{1,0:T(8,128)S(1)} reduce(f32[8,8,128,8]{3,2,1,0:T(8,128)} %reshape.178, f32[]{:T(128)} %constant.53.clone.1), dimensions={1,3}, to_apply=%region_0.0 | reduce | flops 64512 | bytes 266244 | tf_op jit(solution)/shard_map/reduce_sum | solution.py:97
  7.8 1.3 collective-permute-start.6
  9.1 3.0 %collective-permute-start.5 = (f32[3,8,1,128]{3,2,1,0:T(1,128)S(1)}, f32[3,8,1,128]{3,2,1,0:T(1,128)S(1)}, u32[]{:S(2)}, u32[]{:S(2)}) collective-permute-start(f32[3,8,1,128]{3,2,1,0:T(1,128)S(1)} %get-tuple-element.73), channel_id=1, source_target_pairs={{0,8},{8,16},{16,24},{1,9},{9,17},{17,25},{2,10},{10,18},{18,26},{... | collective-permute-start | bytes 36872 | tf_op jit(solution)/shard_map/ppermute | solution.py:23
  12.2 1.3 collective-permute-start.1
  13.5 5.1 %collective-permute-start = (f32[1,8,1,128]{3,2,1,0:T(1,128)S(1)}, f32[1,8,1,128]{3,2,1,0:T(1,128)S(1)}, u32[]{:S(2)}, u32[]{:S(2)}) collective-permute-start(f32[1,8,1,128]{3,2,1,0:T(1,128)S(1)} %get-tuple-element.88), channel_id=1, source_target_pairs={{0,8},{8,16},{16,24},{1,9},{9,17},{17,25},{2,10},{10,18},{18,26},{... | collective-permute-start | bytes 12296 | tf_op jit(solution)/shard_map/ppermute | solution.py:23
  18.6 3.6 %collective-permute-start.22 = (bf16[8,1024]{1,0:T(8,128)(2,1)S(1)}, bf16[8,1024]{1,0:T(8,128)(2,1)S(1)}, u32[]{:S(2)}, u32[]{:S(2)}) collective-permute-start(bf16[8,1024]{1,0:T(8,128)(2,1)S(1)} %get-tuple-element.64), channel_id=1, source_target_pairs={{0,8},{8,16},{16,24},{1,9},{9,17},{17,25},{2,10},{10,18},{18,26},{... | collective-permute-start | bytes 49160 | tf_op jit(solution)/shard_map/ppermute | solution.py:23
  22.7 1.3 collective-permute-start.3
  24.0 4.5 %collective-permute-start.2 = (f32[1,8,10,1]{3,2,1,0:T(8,128)S(1)}, f32[1,8,10,1]{3,2,1,0:T(8,128)S(1)}, u32[]{:S(2)}, u32[]{:S(2)}) collective-permute-start(f32[1,8,10,1]{3,2,1,0:T(8,128)S(1)} %get-tuple-element.75), channel_id=1, source_target_pairs={{0,2},{2,4},{4,6},{1,3},{3,5},{5,7},{8,10},{10,12},{12,14},{9,11},... | collective-permute-start | bytes 968 | tf_op jit(solution)/shard_map/ppermute | solution.py:23
  28.9 1.6 collective-permute-done.2
  30.5 3.4 %collective-permute-start.4 = (f32[1,1,10,130]{3,2,1,0:T(8,128)S(1)}, f32[1,1,10,130]{3,2,1,0:T(8,128)S(1)}, u32[]{:S(2)}, u32[]{:S(2)}) collective-permute-start(f32[1,1,10,130]{3,2,1,0:T(8,128)S(1)} %get-tuple-element.55), channel_id=1, source_target_pairs={{0,1},{2,3},{4,5},{6,7},{8,9},{10,11},{12,13},{14,15},{16,17},{18,... | collective-permute-start | bytes 15608 | tf_op jit(solution)/shard_map/ppermute | solution.py:23
  34.0 1.3 collective-permute-start.10
  35.6 1.3 collective-permute-start.23
  36.9 2.7 %collective-permute-done.10 = f32[1,1,10,130]{3,2,1,0:T(8,128)S(1)} collective-permute-done((f32[1,1,10,130]{3,2,1,0:T(8,128)S(1)}, f32[1,1,10,130]{3,2,1,0:T(8,128)S(1)}, u32[]{:S(2)}, u32[]{:S(2)}) %collective-permute-start.10) | collective-permute-done | bytes 5232 | tf_op jit(solution)/shard_map/ppermute | solution.py:25
  39.6 1.3 collective-permute-start.19
  41.3 3.0 %collective-permute-start.18 = (bf16[8,1024]{1,0:T(8,128)(2,1)S(1)}, bf16[8,1024]{1,0:T(8,128)(2,1)S(1)}, u32[]{:S(2)}, u32[]{:S(2)}) collective-permute-start(bf16[8,1024]{1,0:T(8,128)(2,1)S(1)} %get-tuple-element.61), channel_id=1, source_target_pairs={{0,8},{8,16},{16,24},{1,9},{9,17},{17,25},{2,10},{10,18},{18,26},{... | collective-permute-start | bytes 49160 | tf_op jit(solution)/shard_map/ppermute | solution.py:23
  44.5 1.3 collective-permute-start.8
  45.9 4.9 %collective-permute-start.7 = (f32[3,8,10,1]{3,2,1,0:T(8,128)S(1)}, f32[3,8,10,1]{3,2,1,0:T(8,128)S(1)}, u32[]{:S(2)}, u32[]{:S(2)}) collective-permute-start(f32[3,8,10,1]{3,2,1,0:T(8,128)S(1)} %get-tuple-element.33), channel_id=1, source_target_pairs={{0,2},{2,4},{4,6},{1,3},{3,5},{5,7},{8,10},{10,12},{12,14},{9,11},... | collective-permute-start | bytes 2888 | tf_op jit(solution)/shard_map/ppermute | solution.py:23
  50.9 3.9 %collective-permute-start.24 = (bf16[80,8]{1,0:T(8,128)(2,1)S(1)}, bf16[80,8]{1,0:T(8,128)(2,1)S(1)}, u32[]{:S(2)}, u32[]{:S(2)}) collective-permute-start(bf16[80,8]{1,0:T(8,128)(2,1)S(1)} %get-tuple-element.60), channel_id=1, source_target_pairs={{0,2},{2,4},{4,6},{1,3},{3,5},{5,7},{8,10},{10,12},{12,14},{9,11},... | collective-permute-start | bytes 3848 | tf_op jit(solution)/shard_map/ppermute | solution.py:23
  54.8 1.3 collective-permute-start.25
  56.2 4.5 %collective-permute-start.20 = (bf16[80,8]{1,0:T(8,128)(2,1)S(1)}, bf16[80,8]{1,0:T(8,128)(2,1)S(1)}, u32[]{:S(2)}, u32[]{:S(2)}) collective-permute-start(bf16[80,8]{1,0:T(8,128)(2,1)S(1)} %get-tuple-element.58), channel_id=1, source_target_pairs={{0,2},{2,4},{4,6},{1,3},{3,5},{5,7},{8,10},{10,12},{12,14},{9,11},... | collective-permute-start | bytes 3848 | tf_op jit(solution)/shard_map/ppermute | solution.py:23
  60.8 1.3 collective-permute-start.21
  62.2 2.5 %collective-permute-start.9 = (f32[3,1,10,130]{3,2,1,0:T(8,128)S(1)}, f32[3,1,10,130]{3,2,1,0:T(8,128)S(1)}, u32[]{:S(2)}, u32[]{:S(2)}) collective-permute-start(f32[3,1,10,130]{3,2,1,0:T(8,128)S(1)} %get-tuple-element.25), channel_id=1, source_target_pairs={{0,1},{2,3},{4,5},{6,7},{8,9},{10,11},{12,13},{14,15},{16,17},{18,... | collective-permute-start | bytes 46808 | tf_op jit(solution)/shard_map/ppermute | solution.py:23
  64.7 1.5 collective-permute-start.11
  67.1 0.5 fusion.23
  68.3 0.5 fusion.15
  69.4 0.5 fusion.7
  73.7 0.6 maximum_maximum_fusion
  74.2 1.4 multiply_reduce_fusion.1
  75.7 43.1 %all-reduce = (f32[]{:T(128)}, f32[]{:T(128)}) all-reduce(f32[]{:T(128)} %get-tuple-element.15, f32[]{:T(128)} %get-tuple-element.14), channel_id=1, replica_groups=mesh['gx'=4,'gy'=4,'gz'=2] {'gx','gy','gz'}, use_global_device_ids=true, to_apply=%region_2.3 | all-reduce | flops 2 | bytes 16 | tf_op jit(solution)/shard_map/psum | solution.py:86
  120.1 0.6 multiply_reduce_fusion
  121.2 38.9 %psum.37 = f32[]{:T(128)} all-reduce(f32[]{:T(128)} %multiply_reduce_fusion), channel_id=1, replica_groups=mesh['gx'=4,'gy'=4,'gz'=2] {'gx','gy','gz'}, use_global_device_ids=true, to_apply=%region_6.7 | all-reduce | flops 1 | bytes 8 | tf_op jit(solution)/shard_map/psum | solution.py:86
  161.4 1.3 collective-permute-start.13
  162.7 3.0 %collective-permute-start.12 = (f32[3,8,1,128]{3,2,1,0:T(1,128)S(1)}, f32[3,8,1,128]{3,2,1,0:T(1,128)S(1)}, u32[]{:S(2)}, u32[]{:S(2)}) collective-permute-start(f32[3,8,1,128]{3,2,1,0:T(1,128)S(1)} %get-tuple-element.71), channel_id=1, source_target_pairs={{0,8},{8,16},{16,24},{1,9},{9,17},{17,25},{2,10},{10,18},{18,26},{... | collective-permute-start | bytes 36872 | tf_op jit(solution)/shard_map/ppermute | solution.py:23
  166.8 1.3 collective-permute-start.15
  168.1 4.6 %collective-permute-start.14 = (f32[3,8,10,1]{3,2,1,0:T(8,128)S(1)}, f32[3,8,10,1]{3,2,1,0:T(8,128)S(1)}, u32[]{:S(2)}, u32[]{:S(2)}) collective-permute-start(f32[3,8,10,1]{3,2,1,0:T(8,128)S(1)} %get-tuple-element.31), channel_id=1, source_target_pairs={{0,2},{2,4},{4,6},{1,3},{3,5},{5,7},{8,10},{10,12},{12,14},{9,11},... | collective-permute-start | bytes 2888 | tf_op jit(solution)/shard_map/ppermute | solution.py:23
  172.9 2.3 collective-permute-done.15
  175.2 1.8 collective-permute-done.14
  177.1 5.0 %collective-permute-start.16 = (f32[3,1,10,130]{3,2,1,0:T(8,128)S(1)}, f32[3,1,10,130]{3,2,1,0:T(8,128)S(1)}, u32[]{:S(2)}, u32[]{:S(2)}) collective-permute-start(f32[3,1,10,130]{3,2,1,0:T(8,128)S(1)} %get-tuple-element.21), channel_id=1, source_target_pairs={{0,1},{2,3},{4,5},{6,7},{8,9},{10,11},{12,13},{14,15},{16,17},{18,... | collective-permute-start | bytes 46808 | tf_op jit(solution)/shard_map/ppermute | solution.py:23
  182.2 1.5 collective-permute-start.17
  184.0 4.2 %collective-permute-done.17 = f32[3,1,10,130]{3,2,1,0:T(8,128)S(1)} collective-permute-done((f32[3,1,10,130]{3,2,1,0:T(8,128)S(1)}, f32[3,1,10,130]{3,2,1,0:T(8,128)S(1)}, u32[]{:S(2)}, u32[]{:S(2)}) %collective-permute-start.17) | collective-permute-done | bytes 15632 | tf_op jit(solution)/shard_map/ppermute | solution.py:25
  188.2 0.6 maximum_maximum_fusion.1
  188.8 1.4 fusion.66
  190.3 41.3 %psum.38 = f32[]{:T(128)} all-reduce(f32[]{:T(128)} %fusion.66), channel_id=1, replica_groups=mesh['gx'=4,'gy'=4,'gz'=2] {'gx','gy','gz'}, use_global_device_ids=true, to_apply=%region_8.9 | all-reduce | flops 1 | bytes 8 | tf_op jit(solution)/shard_map/psum | solution.py:106
  233.0 5.4 %psum.39 = f32[8,128]{1,0:T(8,128)S(1)} all-reduce(f32[8,128]{1,0:T(8,128)S(1)} %fusion.254), channel_id=1, replica_groups=mesh['gx'=4,'gy'=4,'gz'=2] {'gz'}, use_global_device_ids=true, to_apply=%region_9.10 | all-reduce | flops 1024 | bytes 8192 | tf_op jit(solution)/shard_map/psum | solution.py:34
  238.4 2.5 %broadcast_in_dim.75 = f32[8,8,128,8]{3,2,1,0:T(8,128)} broadcast(f32[8,128]{1,0:T(8,128)S(1)} %broadcast_multiply_fusion), dimensions={0,2} | broadcast | bytes 266240 | tf_op jit(solution)/shard_map/broadcast_in_dim | solution.py:114
  240.9 4.0 %mul.988 = f32[64,1024]{1,0:T(8,128)S(1)} reshape(f32[8,8,128,8]{3,2,1,0:T(8,128)} %broadcast_in_dim.75) | data formatting | bytes 524288 | tf_op jit(solution)/shard_map/mul | solution.py:137
  244.9 0.8 dynamic-slice_add_fusion
  (104 shorter events, 10.0 us)
Async XLA Ops:
  0.6 7.1 %copy-start = (f32[3,8,8,128]{3,2,1,0:T(8,128)S(1)}, f32[3,8,8,128]{3,2,1,0:T(8,128)}, u32[]{:S(2)}) copy-start(f32[3,8,8,128]{3,2,1,0:T(8,128)} %param.6) | copy-start | bytes 294916
  0.6 11.5 %copy-start.1 = (f32[8,8,128]{2,1,0:T(8,128)S(1)}, f32[8,8,128]{2,1,0:T(8,128)}, u32[]{:S(2)}) copy-start(f32[8,8,128]{2,1,0:T(8,128)} %param.7) | copy-start | bytes 98308
  0.7 17.9 %copy-start.3 = (bf16[64,1024]{1,0:T(8,128)(2,1)S(1)}, bf16[64,1024]{1,0:T(8,128)(2,1)}, u32[]{:S(2)}) copy-start(bf16[64,1024]{1,0:T(8,128)(2,1)} %param.9) | copy-start | bytes 393220
  0.7 21.6 %copy-start.2 = (f32[64,1024]{1,0:T(8,128)S(1)}, f32[64,1024]{1,0:T(8,128)}, u32[]{:S(2)}) copy-start(f32[64,1024]{1,0:T(8,128)} %param.8) | copy-start | bytes 786436
  7.8 33.5 %collective-permute-start.6 = (f32[3,8,1,128]{3,2,1,0:T(1,128)S(1)}, f32[3,8,1,128]{3,2,1,0:T(1,128)S(1)}, u32[]{:S(2)}, u32[]{:S(2)}) collective-permute-start(f32[3,8,1,128]{3,2,1,0:T(1,128)S(1)} %get-tuple-element.74), channel_id=1, source_target_pairs={{8,0},{16,8},{24,16},{9,1},{17,9},{25,17},{10,2},{18,10},{26,18},{... | collective-permute-start | bytes 36872 | tf_op jit(solution)/shard_map/ppermute | solution.py:25
  9.1 35.2 %collective-permute-start.5 = (f32[3,8,1,128]{3,2,1,0:T(1,128)S(1)}, f32[3,8,1,128]{3,2,1,0:T(1,128)S(1)}, u32[]{:S(2)}, u32[]{:S(2)}) collective-permute-start(f32[3,8,1,128]{3,2,1,0:T(1,128)S(1)} %get-tuple-element.73), channel_id=1, source_target_pairs={{0,8},{8,16},{16,24},{1,9},{9,17},{17,25},{2,10},{10,18},{18,26},{... | collective-permute-start | bytes 36872 | tf_op jit(solution)/shard_map/ppermute | solution.py:23
  12.2 10.4 %collective-permute-start.1 = (f32[1,8,1,128]{3,2,1,0:T(1,128)S(1)}, f32[1,8,1,128]{3,2,1,0:T(1,128)S(1)}, u32[]{:S(2)}, u32[]{:S(2)}) collective-permute-start(f32[1,8,1,128]{3,2,1,0:T(1,128)S(1)} %get-tuple-element.89), channel_id=1, source_target_pairs={{8,0},{16,8},{24,16},{9,1},{17,9},{25,17},{10,2},{18,10},{26,18},{... | collective-permute-start | bytes 12296 | tf_op jit(solution)/shard_map/ppermute | solution.py:25
  13.5 9.1 %collective-permute-start = (f32[1,8,1,128]{3,2,1,0:T(1,128)S(1)}, f32[1,8,1,128]{3,2,1,0:T(1,128)S(1)}, u32[]{:S(2)}, u32[]{:S(2)}) collective-permute-start(f32[1,8,1,128]{3,2,1,0:T(1,128)S(1)} %get-tuple-element.88), channel_id=1, source_target_pairs={{0,8},{8,16},{16,24},{1,9},{9,17},{17,25},{2,10},{10,18},{18,26},{... | collective-permute-start | bytes 12296 | tf_op jit(solution)/shard_map/ppermute | solution.py:23
  18.6 27.2 %collective-permute-start.22 = (bf16[8,1024]{1,0:T(8,128)(2,1)S(1)}, bf16[8,1024]{1,0:T(8,128)(2,1)S(1)}, u32[]{:S(2)}, u32[]{:S(2)}) collective-permute-start(bf16[8,1024]{1,0:T(8,128)(2,1)S(1)} %get-tuple-element.64), channel_id=1, source_target_pairs={{0,8},{8,16},{16,24},{1,9},{9,17},{17,25},{2,10},{10,18},{18,26},{... | collective-permute-start | bytes 49160 | tf_op jit(solution)/shard_map/ppermute | solution.py:23
  22.7 6.2 %collective-permute-start.3 = (f32[1,8,10,1]{3,2,1,0:T(8,128)S(1)}, f32[1,8,10,1]{3,2,1,0:T(8,128)S(1)}, u32[]{:S(2)}, u32[]{:S(2)}) collective-permute-start(f32[1,8,10,1]{3,2,1,0:T(8,128)S(1)} %get-tuple-element.76), channel_id=1, source_target_pairs={{2,0},{4,2},{6,4},{3,1},{5,3},{7,5},{10,8},{12,10},{14,12},{11,9},... | collective-permute-start | bytes 968 | tf_op jit(solution)/shard_map/ppermute | solution.py:25
  24.0 6.4 %collective-permute-start.2 = (f32[1,8,10,1]{3,2,1,0:T(8,128)S(1)}, f32[1,8,10,1]{3,2,1,0:T(8,128)S(1)}, u32[]{:S(2)}, u32[]{:S(2)}) collective-permute-start(f32[1,8,10,1]{3,2,1,0:T(8,128)S(1)} %get-tuple-element.75), channel_id=1, source_target_pairs={{0,2},{2,4},{4,6},{1,3},{3,5},{5,7},{8,10},{10,12},{12,14},{9,11},... | collective-permute-start | bytes 968 | tf_op jit(solution)/shard_map/ppermute | solution.py:23
  30.5 5.0 %collective-permute-start.4 = (f32[1,1,10,130]{3,2,1,0:T(8,128)S(1)}, f32[1,1,10,130]{3,2,1,0:T(8,128)S(1)}, u32[]{:S(2)}, u32[]{:S(2)}) collective-permute-start(f32[1,1,10,130]{3,2,1,0:T(8,128)S(1)} %get-tuple-element.55), channel_id=1, source_target_pairs={{0,1},{2,3},{4,5},{6,7},{8,9},{10,11},{12,13},{14,15},{16,17},{18,... | collective-permute-start | bytes 15608 | tf_op jit(solution)/shard_map/ppermute | solution.py:23
  34.0 5.6 %collective-permute-start.10 = (f32[1,1,10,130]{3,2,1,0:T(8,128)S(1)}, f32[1,1,10,130]{3,2,1,0:T(8,128)S(1)}, u32[]{:S(2)}, u32[]{:S(2)}) collective-permute-start(f32[1,1,10,130]{3,2,1,0:T(8,128)S(1)} %get-tuple-element.56), channel_id=1, source_target_pairs={{1,0},{3,2},{5,4},{7,6},{9,8},{11,10},{13,12},{15,14},{17,16},{19,... | collective-permute-start | bytes 15608 | tf_op jit(solution)/shard_map/ppermute | solution.py:25
  35.6 15.2 %collective-permute-start.23 = (bf16[8,1024]{1,0:T(8,128)(2,1)S(1)}, bf16[8,1024]{1,0:T(8,128)(2,1)S(1)}, u32[]{:S(2)}, u32[]{:S(2)}) collective-permute-start(bf16[8,1024]{1,0:T(8,128)(2,1)S(1)} %get-tuple-element.63), channel_id=1, source_target_pairs={{8,0},{16,8},{24,16},{9,1},{17,9},{25,17},{10,2},{18,10},{26,18},{... | collective-permute-start | bytes 49160 | tf_op jit(solution)/shard_map/ppermute | solution.py:25
  39.6 15.2 %collective-permute-start.19 = (bf16[8,1024]{1,0:T(8,128)(2,1)S(1)}, bf16[8,1024]{1,0:T(8,128)(2,1)S(1)}, u32[]{:S(2)}, u32[]{:S(2)}) collective-permute-start(bf16[8,1024]{1,0:T(8,128)(2,1)S(1)} %get-tuple-element.62), channel_id=1, source_target_pairs={{8,0},{16,8},{24,16},{9,1},{17,9},{25,17},{10,2},{18,10},{26,18},{... | collective-permute-start | bytes 49160 | tf_op jit(solution)/shard_map/ppermute | solution.py:25
  41.3 14.8 %collective-permute-start.18 = (bf16[8,1024]{1,0:T(8,128)(2,1)S(1)}, bf16[8,1024]{1,0:T(8,128)(2,1)S(1)}, u32[]{:S(2)}, u32[]{:S(2)}) collective-permute-start(bf16[8,1024]{1,0:T(8,128)(2,1)S(1)} %get-tuple-element.61), channel_id=1, source_target_pairs={{0,8},{8,16},{16,24},{1,9},{9,17},{17,25},{2,10},{10,18},{18,26},{... | collective-permute-start | bytes 49160 | tf_op jit(solution)/shard_map/ppermute | solution.py:23
  44.5 16.2 %collective-permute-start.8 = (f32[3,8,10,1]{3,2,1,0:T(8,128)S(1)}, f32[3,8,10,1]{3,2,1,0:T(8,128)S(1)}, u32[]{:S(2)}, u32[]{:S(2)}) collective-permute-start(f32[3,8,10,1]{3,2,1,0:T(8,128)S(1)} %get-tuple-element.34), channel_id=1, source_target_pairs={{2,0},{4,2},{6,4},{3,1},{5,3},{7,5},{10,8},{12,10},{14,12},{11,9},... | collective-permute-start | bytes 2888 | tf_op jit(solution)/shard_map/ppermute | solution.py:25
  45.9 16.2 %collective-permute-start.7 = (f32[3,8,10,1]{3,2,1,0:T(8,128)S(1)}, f32[3,8,10,1]{3,2,1,0:T(8,128)S(1)}, u32[]{:S(2)}, u32[]{:S(2)}) collective-permute-start(f32[3,8,10,1]{3,2,1,0:T(8,128)S(1)} %get-tuple-element.33), channel_id=1, source_target_pairs={{0,2},{2,4},{4,6},{1,3},{3,5},{5,7},{8,10},{10,12},{12,14},{9,11},... | collective-permute-start | bytes 2888 | tf_op jit(solution)/shard_map/ppermute | solution.py:23
  50.9 13.8 %collective-permute-start.24 = (bf16[80,8]{1,0:T(8,128)(2,1)S(1)}, bf16[80,8]{1,0:T(8,128)(2,1)S(1)}, u32[]{:S(2)}, u32[]{:S(2)}) collective-permute-start(bf16[80,8]{1,0:T(8,128)(2,1)S(1)} %get-tuple-element.60), channel_id=1, source_target_pairs={{0,2},{2,4},{4,6},{1,3},{3,5},{5,7},{8,10},{10,12},{12,14},{9,11},... | collective-permute-start | bytes 3848 | tf_op jit(solution)/shard_map/ppermute | solution.py:23
  54.8 11.4 %collective-permute-start.25 = (bf16[80,8]{1,0:T(8,128)(2,1)S(1)}, bf16[80,8]{1,0:T(8,128)(2,1)S(1)}, u32[]{:S(2)}, u32[]{:S(2)}) collective-permute-start(bf16[80,8]{1,0:T(8,128)(2,1)S(1)} %get-tuple-element.59), channel_id=1, source_target_pairs={{2,0},{4,2},{6,4},{3,1},{5,3},{7,5},{10,8},{12,10},{14,12},{11,9},... | collective-permute-start | bytes 3848 | tf_op jit(solution)/shard_map/ppermute | solution.py:25
  56.2 10.2 %collective-permute-start.20 = (bf16[80,8]{1,0:T(8,128)(2,1)S(1)}, bf16[80,8]{1,0:T(8,128)(2,1)S(1)}, u32[]{:S(2)}, u32[]{:S(2)}) collective-permute-start(bf16[80,8]{1,0:T(8,128)(2,1)S(1)} %get-tuple-element.58), channel_id=1, source_target_pairs={{0,2},{2,4},{4,6},{1,3},{3,5},{5,7},{8,10},{10,12},{12,14},{9,11},... | collective-permute-start | bytes 3848 | tf_op jit(solution)/shard_map/ppermute | solution.py:23
  60.8 5.7 %collective-permute-start.21 = (bf16[80,8]{1,0:T(8,128)(2,1)S(1)}, bf16[80,8]{1,0:T(8,128)(2,1)S(1)}, u32[]{:S(2)}, u32[]{:S(2)}) collective-permute-start(bf16[80,8]{1,0:T(8,128)(2,1)S(1)} %get-tuple-element.57), channel_id=1, source_target_pairs={{2,0},{4,2},{6,4},{3,1},{5,3},{7,5},{10,8},{12,10},{14,12},{11,9},... | collective-permute-start | bytes 3848 | tf_op jit(solution)/shard_map/ppermute | solution.py:25
  62.2 11.4 %collective-permute-start.9 = (f32[3,1,10,130]{3,2,1,0:T(8,128)S(1)}, f32[3,1,10,130]{3,2,1,0:T(8,128)S(1)}, u32[]{:S(2)}, u32[]{:S(2)}) collective-permute-start(f32[3,1,10,130]{3,2,1,0:T(8,128)S(1)} %get-tuple-element.25), channel_id=1, source_target_pairs={{0,1},{2,3},{4,5},{6,7},{8,9},{10,11},{12,13},{14,15},{16,17},{18,... | collective-permute-start | bytes 46808 | tf_op jit(solution)/shard_map/ppermute | solution.py:23
  64.7 8.9 %collective-permute-start.11 = (f32[3,1,10,130]{3,2,1,0:T(8,128)S(1)}, f32[3,1,10,130]{3,2,1,0:T(8,128)S(1)}, u32[]{:S(2)}, u32[]{:S(2)}) collective-permute-start(f32[3,1,10,130]{3,2,1,0:T(8,128)S(1)} %get-tuple-element.26), channel_id=1, source_target_pairs={{1,0},{3,2},{5,4},{7,6},{9,8},{11,10},{13,12},{15,14},{17,16},{19,... | collective-permute-start | bytes 46808 | tf_op jit(solution)/shard_map/ppermute | solution.py:25
  161.4 4.7 %collective-permute-start.13 = (f32[3,8,1,128]{3,2,1,0:T(1,128)S(1)}, f32[3,8,1,128]{3,2,1,0:T(1,128)S(1)}, u32[]{:S(2)}, u32[]{:S(2)}) collective-permute-start(f32[3,8,1,128]{3,2,1,0:T(1,128)S(1)} %get-tuple-element.72), channel_id=1, source_target_pairs={{8,0},{16,8},{24,16},{9,1},{17,9},{25,17},{10,2},{18,10},{26,18},{... | collective-permute-start | bytes 36872 | tf_op jit(solution)/shard_map/ppermute | solution.py:25
  162.7 3.9 %collective-permute-start.12 = (f32[3,8,1,128]{3,2,1,0:T(1,128)S(1)}, f32[3,8,1,128]{3,2,1,0:T(1,128)S(1)}, u32[]{:S(2)}, u32[]{:S(2)}) collective-permute-start(f32[3,8,1,128]{3,2,1,0:T(1,128)S(1)} %get-tuple-element.71), channel_id=1, source_target_pairs={{0,8},{8,16},{16,24},{1,9},{9,17},{17,25},{2,10},{10,18},{18,26},{... | collective-permute-start | bytes 36872 | tf_op jit(solution)/shard_map/ppermute | solution.py:23
  166.8 8.5 %collective-permute-start.15 = (f32[3,8,10,1]{3,2,1,0:T(8,128)S(1)}, f32[3,8,10,1]{3,2,1,0:T(8,128)S(1)}, u32[]{:S(2)}, u32[]{:S(2)}) collective-permute-start(f32[3,8,10,1]{3,2,1,0:T(8,128)S(1)} %get-tuple-element.32), channel_id=1, source_target_pairs={{2,0},{4,2},{6,4},{3,1},{5,3},{7,5},{10,8},{12,10},{14,12},{11,9},... | collective-permute-start | bytes 2888 | tf_op jit(solution)/shard_map/ppermute | solution.py:25
  168.1 8.9 %collective-permute-start.14 = (f32[3,8,10,1]{3,2,1,0:T(8,128)S(1)}, f32[3,8,10,1]{3,2,1,0:T(8,128)S(1)}, u32[]{:S(2)}, u32[]{:S(2)}) collective-permute-start(f32[3,8,10,1]{3,2,1,0:T(8,128)S(1)} %get-tuple-element.31), channel_id=1, source_target_pairs={{0,2},{2,4},{4,6},{1,3},{3,5},{5,7},{8,10},{10,12},{12,14},{9,11},... | collective-permute-start | bytes 2888 | tf_op jit(solution)/shard_map/ppermute | solution.py:23
  177.1 6.9 %collective-permute-start.16 = (f32[3,1,10,130]{3,2,1,0:T(8,128)S(1)}, f32[3,1,10,130]{3,2,1,0:T(8,128)S(1)}, u32[]{:S(2)}, u32[]{:S(2)}) collective-permute-start(f32[3,1,10,130]{3,2,1,0:T(8,128)S(1)} %get-tuple-element.21), channel_id=1, source_target_pairs={{0,1},{2,3},{4,5},{6,7},{8,9},{10,11},{12,13},{14,15},{16,17},{18,... | collective-permute-start | bytes 46808 | tf_op jit(solution)/shard_map/ppermute | solution.py:23
  182.2 6.0 %collective-permute-start.17 = (f32[3,1,10,130]{3,2,1,0:T(8,128)S(1)}, f32[3,1,10,130]{3,2,1,0:T(8,128)S(1)}, u32[]{:S(2)}, u32[]{:S(2)}) collective-permute-start(f32[3,1,10,130]{3,2,1,0:T(8,128)S(1)} %get-tuple-element.22), channel_id=1, source_target_pairs={{1,0},{3,2},{5,4},{7,6},{9,8},{11,10},{13,12},{15,14},{17,16},{19,... | collective-permute-start | bytes 46808 | tf_op jit(solution)/shard_map/ppermute | solution.py:25
  233.0 11.9 %copy-start.4 = (f32[3,8,8,128]{3,2,1,0:T(8,128)}, f32[3,8,8,128]{3,2,1,0:T(8,128)S(1)}, u32[]{:S(2)}) copy-start(f32[3,8,8,128]{3,2,1,0:T(8,128)S(1)} %multiply_add_fusion) | copy-start | bytes 294916
where the time goes:
time: 247 us; the launch traced here: 246 us
  blocking collectives  129 us (52%)
  starting transfers between devices  68.4 us (28%)
  other arithmetic  17.3 us (7%)
  waiting for transfers between devices  13.3 us (5%)
  local copies, waits for them, and re-layouts  12.5 us (5%)
  between operations  5.53 us (2%)
    psum x2, blocking collectives, squares(): return lax.psum(jnp.sum(residual * residual), ('gx', 'gy', 'gz'))  82 us
    ppermute x13, starting transfers between devices, extended_2(): lax.ppermute(tail, axis, [(i, (i + 1) % count) for i in range(ends)])  51.2 us
    psum x1, blocking collectives, local(): alpha = norm_now / lax.psum(jnp.sum(direction * image), ('gx', 'gy', 'gz'))  41.3 us
    ppermute x13, starting transfers between devices, extended_2(): lax.ppermute(head, axis, [((i + 1) % count, i) for i in range(ends)])  17.2 us
    ppermute x13, waiting for transfers between devices, extended_2(): lax.ppermute(head, axis, [((i + 1) % count, i) for i in range(ends)])  9.47 us
    psum x1, blocking collectives, spread(): return lax.psum(block, axis)  5.37 us
  transfers between devices with their start and end apart: 26, of which 7 were waited for; matrix products, arithmetic and copies ran while one was open for 4% of the time, Pallas kernels for 0%

commit v1 on v0

v1 whole, which is shorter than its diff:
```python
import functools

import jax
import jax.numpy as jnp
from jax import lax
from jax.experimental import pallas as pl
from jax.experimental.pallas import tpu as pltpu
from jax.sharding import PartitionSpec as P

STEPS = 8
REACH = 2

drag = 1.0
time_step = 1.0
load_gain = 4.0

W_FACE = 0.5
W_EDGE = 0.25
W_CORNER = 0.5 / 3.0
W_ALL = 6 * W_FACE + 12 * W_EDGE + 8 * W_CORNER

MESH = pl.DeviceIdType.MESH
HIGH = lax.Precision.HIGHEST
SIGNS = (-1, 0, 1)
OFFSETS = [(a, b, c) for a in SIGNS for b in SIGNS for c in SIGNS if (a, b, c) != (0, 0, 0)]


def side(sign):
    return 0 if sign < 0 else 1


def code(a, b, c):
    return (a + 1) * 9 + (b + 1) * 3 + (c + 1)


def weighted(u):
    rows, lanes = u.shape[1:]
    beside = pltpu.roll(u, 1, 2) + pltpu.roll(u, lanes - 1, 2)
    near = beside + pltpu.roll(u, 1, 1) + pltpu.roll(u, rows - 1, 1)
    diagonal = pltpu.roll(beside, 1, 1) + pltpu.roll(beside, rows - 1, 1)
    same = W_FACE * near + W_EDGE * diagonal
    other = W_FACE * u + W_EDGE * near + W_CORNER * diagonal
    return same[1:-1] + other[:-2] + other[2:]


def total(x):
    x = x.reshape((-1,) + x.shape[-2:]).sum(axis=0)
    return x.sum(axis=(0, 1), keepdims=True)


def kernel(
    sizes,
    force_hbm,
    visc_hbm,
    topo_hbm,
    kappa_hbm,
    velocity_ref,
    surface_ref,
    field,
    lane_pack,
    row_pack,
    from_depth,
    from_rows,
    from_rows_depth,
    from_cols,
    ext,
    image,
    height,
    conduct,
    work,
    face_right,
    face_down,
    inside,
    row_out,
    gathered,
    top_own,
    top_in,
    load_sem,
    rim_send,
    rim_recv,
    surf_send,
    surf_recv,
    sum_send,
    sum_recv,
    top_send,
    top_recv,
):
    nx, ny, nz = sizes
    count = nx * ny * nz
    x, y, z = lax.axis_index("gx"), lax.axis_index("gy"), lax.axis_index("gz")
    depth, cells, width = field.shape[1:]
    rows, cols = topo_hbm.shape
    share = cols // nz
    krow = 16

    xs = [lax.rem(x + k, nx) for k in range(nx)]
    ys = [lax.rem(y + k, ny) for k in range(ny)]
    zs = [lax.rem(z + k, nz) for k in range(nz)]
    others = [(a, b, c) for a in range(nx) for b in range(ny) for c in range(nz)][1:]
    others.sort(key=lambda o: -(min(o[0], nx - o[0]) + min(o[1], ny - o[1]) + min(o[2], nz - o[2])))
    is_top = z == nz - 1

    loads = [
        pltpu.make_async_copy(topo_hbm, height.at[STEPS : STEPS + rows, width : width + cols], load_sem.at[0]),
        pltpu.make_async_copy(force_hbm, field.at[0:3], load_sem.at[1]),
        pltpu.make_async_copy(visc_hbm, field.at[3], load_sem.at[2]),
        pltpu.make_async_copy(kappa_hbm, conduct.at[krow : krow + rows, width : width + cols], load_sem.at[3]),
    ]
    for copy in loads:
        copy.start()

    for ref in (from_depth, from_rows, from_rows_depth, from_cols):
        ref[...] = jnp.zeros_like(ref)
    height[0:STEPS, :] = jnp.zeros((STEPS, height.shape[1]), height.dtype)
    height[STEPS + rows :, :] = jnp.zeros((STEPS, height.shape[1]), height.dtype)
    height[STEPS : STEPS + rows, 0:width] = jnp.zeros((rows, width), height.dtype)
    height[STEPS : STEPS + rows, width + cols :] = jnp.zeros((rows, width), height.dtype)
    conduct[0:krow, :] = jnp.zeros((krow, conduct.shape[1]), conduct.dtype)
    conduct[krow + rows :, :] = jnp.zeros((krow, conduct.shape[1]), conduct.dtype)
    conduct[krow : krow + rows, 0:width] = jnp.zeros((rows, width), conduct.dtype)
    conduct[krow : krow + rows, width + cols :] = jnp.zeros((rows, width), conduct.dtype)

    barrier = pltpu.get_barrier_semaphore()
    for a, b, c in others:
        pl.semaphore_signal(barrier, inc=1, device_id=(xs[a], ys[b], zs[c]), device_id_type=MESH)

    loads[0].wait()
    ratio_r, ratio_c = rows // cells, cols // width
    by_rows = height[STEPS : STEPS + rows, width : width + cols].reshape(cells, ratio_r, cols).sum(axis=1)
    at = lax.broadcasted_iota(jnp.int32, (cols, width), 0)
    first = lax.broadcasted_iota(jnp.int32, (cols, width), 1) * ratio_c
    pick = jnp.where((at >= first) & (at < first + ratio_c), 1.0, 0.0)
    load = jnp.dot(by_rows, pick, precision=HIGH, preferred_element_type=jnp.float32) / (ratio_r * ratio_c)
    loads[1].wait()
    loads[2].wait()
    field[2, depth - 1] = field[2, depth - 1] + jnp.where(is_top, -load_gain * load, 0.0)

    lane = lax.broadcasted_iota(jnp.int32, (cells, width), 1)
    sub = lax.broadcasted_iota(jnp.int32, (cells, width), 0)
    packed = jnp.zeros((cells, width), jnp.float32)
    up_pack, down_pack = {}, {}
    for f in range(4):
        for d in range(depth):
            tile = field[f, d]
            j = f * depth + d
            packed = jnp.where((lane >= 4 * j) & (lane < 4 * j + 4), pltpu.roll(tile, (4 * j + 2) % width, 1), packed)
            t, p = (d // 2) * 2 + f // 2, (d % 2) * 2 + f % 2
            chosen = (sub >= 2 * p) & (sub < 2 * p + 2)
            up = pltpu.roll(tile, (2 * p) % 8, 0) if p else tile
            down = pltpu.roll(tile, (2 * p + 2) % 8, 0) if (2 * p + 2) % 8 else tile
            up_pack[t] = jnp.where(chosen, up, up_pack.get(t, 0.0))
            down_pack[t] = jnp.where(chosen, down, down_pack.get(t, 0.0))
    lane_pack[...] = packed
    for t in range(depth):
        row_pack[0, t] = up_pack[t]
        row_pack[1, t] = down_pack[t]

    def present(a, b, c):
        yes = None
        for sign, at_, size in ((a, z, nz), (b, x, nx), (c, y, ny)):
            if sign:
                one = at_ > 0 if sign < 0 else at_ < size - 1
                yes = one if yes is None else jnp.logical_and(yes, one)
        return yes

    def rim_copy(a, b, c):
        span = slice(depth - 2, depth) if a > 0 else slice(0, 2)
        if c != 0:
            src, dst = lane_pack, from_cols.at[(1 - a) * 3 + (1 - b), side(-c)]
        elif b == 0:
            src, dst = field.at[:, span], from_depth.at[side(-a)]
        elif a == 0:
            src, dst = row_pack.at[side(b)], from_rows.at[side(-b)]
        else:
            src, dst = row_pack.at[side(b), span], from_rows_depth.at[side(-a), side(-b)]
        return pltpu.make_async_remote_copy(
            src_ref=src,
            dst_ref=dst,
            send_sem=rim_send.at[code(a, b, c)],
            recv_sem=rim_recv.at[code(-a, -b, -c)],
            device_id=(x + b, y + c, z + a),
            device_id_type=MESH,
        )

    pl.semaphore_wait(barrier, count - 1)
    for o in OFFSETS:
        pl.when(present(*o))(lambda o=o: rim_copy(*o).start())

    surf_offsets = [(b, c) for b in SIGNS for c in SIGNS if (b, c) != (0, 0)]

    def surf_present(b, c, receiving):
        yes = present(0, b, c)
        toward = -c if receiving else c
        if toward > 0:
            yes = jnp.logical_and(yes, z == 0)
        if toward < 0:
            yes = jnp.logical_and(yes, z == nz - 1)
        return yes

    def surf_copies(b, c):
        def spans(sign, size, halo, lead):
            if sign == 0:
                return slice(0, size), slice(lead, lead + size)
            if sign > 0:
                return slice(size - halo, size), slice(0, halo)
            return slice(0, halo), slice(lead + size, lead + size + halo)

        cs, cd = spans(c, cols, width, width)
        n = (b + 1) * 3 + (c + 1)
        m = (1 - b) * 3 + (1 - c)
        made = []
        for i, (src, dst, halo) in enumerate(((topo_hbm, height, STEPS), (kappa_hbm, conduct, krow))):
            rs, rd = spans(b, rows, halo, halo)
            made.append(
                pltpu.make_async_remote_copy(
                    src_ref=src.at[rs, cs],
                    dst_ref=dst.at[rd, cd],
                    send_sem=surf_send.at[i, n],
                    recv_sem=surf_recv.at[i, m],
                    device_id=(x + b, y + c, z),
                    device_id_type=MESH,
                )
            )
        return made

    def surf_start(b, c):
        for copy in surf_copies(b, c):
            copy.start()

    for o in surf_offsets:
        pl.when(surf_present(*o, False))(lambda o=o: surf_start(*o))

    for a, b, c in OFFSETS:
        pl.when(present(a, b, c))(lambda o=(-a, -b, -c): rim_copy(*o).wait_recv())
    from_low = sub < cells // 2
    from_left = (lane % 4) < 2
    for a in SIGNS:
        joined = []
        low = from_cols[(a + 1) * 3 + 1, 0]
        high = from_cols[(a + 1) * 3 + 1, 1]
        if True:
            joined.append(jnp.where(from_left, low, high))
            low = jnp.where(from_low, from_cols[(a + 1) * 3 + 2, 0], from_cols[(a + 1) * 3, 0])
            high = jnp.where(from_low, from_cols[(a + 1) * 3 + 2, 1], from_cols[(a + 1) * 3, 1])
            joined.append(jnp.where(from_left, low, high))
        for f in range(4):
            for d in range(depth) if a == 0 else (range(2) if a > 0 else range(depth - 2, depth)):
                layer = REACH + a * depth + d
                t, p = (d // 2) * 2 + f // 2, (d % 2) * 2 + f % 2
                if a == 0:
                    center, above, below = field[f, d], from_rows[0, t], from_rows[1, t]
                else:
                    center = from_depth[side(a), f, d % 2]
                    above = from_rows_depth[side(a), 0, f // 2]
                    below = from_rows_depth[side(a), 1, f // 2]
                above = pltpu.roll(above, 6 - 2 * p, 0) if p != 3 else above
                below = pltpu.roll(below, 8 - 2 * p, 0) if p else below
                j = f * depth + d
                ext[f, layer, 0:cells, 0:width] = center
                ext[f, layer, cells:, 0:width] = jnp.where(from_low, below, above)
                turn = (width - 2 - 4 * j) % width
                for r in range(2):
                    tile = pltpu.roll(joined[r], turn, 1) if turn else joined[r]
                    ext[f, layer, r * cells : (r + 1) * cells, width:] = tile

    eta = ext[3]
    gain = drag + W_ALL * eta[1:-1] + weighted(eta)
    for f in range(3):
        v = ext[f]
        out = gain * v[1:-1] - eta[1:-1] * weighted(v) - weighted(eta * v)
        image[f] = jnp.where(eta[1:-1] > 0.0, out, 0.0)
    eta1 = eta[1:-1]
    center = (slice(None), slice(0, cells), slice(0, width))
    m0 = m1 = jnp.zeros((cells, width), jnp.float32)
    for f in range(3):
        b = field[f]
        ab = image[f, 1:-1, 0:cells, 0:width]
        m0 = m0 + (b * b).sum(axis=0)
        m1 = m1 + (b * ab).sum(axis=0)
    m0, m1 = total(m0), total(m1)
    own = jnp.where(m0 > 0.0, m1 / m0, 0.0)
    sums = [jnp.zeros((cells, width), jnp.float32) for _ in range(4)]
    for f in range(3):
        v = image[f]
        b = field[f]
        ab = v[1:-1][center]
        again = (
            gain[1:-1][center] * ab
            - eta1[1:-1][center] * weighted(v)[center]
            - weighted(eta1 * v)[center]
        )
        w = ab - own * b
        aw = again - own * ab
        for i, (p, q) in enumerate(((w, b), (w, w), (w, aw), (b, aw))):
            sums[i] = sums[i] + (p * q).sum(axis=0)
    numbers = [m0, m1, own] + [total(s) for s in sums]
    spot = lax.broadcasted_iota(jnp.int32, (1, width), 1)
    line = jnp.zeros((1, width), jnp.float32)
    for i, number in enumerate(numbers):
        line = jnp.where(spot == i, number, line)
    row_out[0] = line
    me = (x * ny + y) * nz + z
    gathered[me] = line
    top_own[0] = field[2, depth - 1]
    top_own[1] = image[2, depth, 0:cells, 0:width]
    for a, b, c in others:
        pltpu.make_async_remote_copy(
            src_ref=row_out.at[0],
            dst_ref=gathered.at[me],
            send_sem=sum_send,
            recv_sem=sum_recv,
            device_id=(xs[a], ys[b], zs[c]),
            device_id_type=MESH,
        ).start()

    def top_copy(k):
        return pltpu.make_async_remote_copy(
            src_ref=top_own,
            dst_ref=top_in,
            send_sem=top_send.at[k],
            recv_sem=top_recv,
            device_id=(x, y, zs[k]),
            device_id_type=MESH,
        )

    @pl.when(is_top)
    def _():
        for k in range(1, nz):
            top_copy(k).start()

    for b, c in surf_offsets:

        def arrived(b=b, c=c):
            for copy in surf_copies(-b, -c):
                copy.wait_recv()

        pl.when(surf_present(b, c, True))(arrived)
    loads[3].wait()
    start = pl.multiple_of(z * share, share)
    tall = rows + 2 * STEPS
    left_half = lax.broadcasted_iota(jnp.int32, (1, width), 1) < width // 2

    def joined_window(ref):
        wide = ref[:, pl.ds(start, share + 2 * width)].astype(jnp.float32)
        rim = jnp.where(left_half, wide[:, width + share :], wide[:, :width])
        return jnp.concatenate([wide[:, width : width + share], rim], axis=1)

    work[...] = joined_window(height)
    k = joined_window(conduct)[krow - STEPS : krow + rows + STEPS]
    span = share + width
    face_right[...] = 0.5 * (k + pltpu.roll(k, span - 1, 1))
    face_down[...] = 0.5 * (k + pltpu.roll(k, tall - 1, 0))
    row_at = x * rows - STEPS + lax.broadcasted_iota(jnp.int32, (tall, span), 0)
    lane_at = lax.broadcasted_iota(jnp.int32, (tall, span), 1)
    lane_at = jnp.where(lane_at >= span - width // 2, lane_at - span, lane_at)
    col_at = y * cols + z * share + lane_at
    inside[...] = jnp.where(
        (row_at >= 0) & (row_at < rows * nx) & (col_at >= 0) & (col_at < cols * ny), time_step, 0.0
    )

    def diffuse(_, carry):
        h = work[...]
        s = pltpu.roll(h, span - 1, 1) - h
        along = face_right[...] * s * lax.rsqrt(1.0 + s * s)
        s = pltpu.roll(h, tall - 1, 0) - h
        across = face_down[...] * s * lax.rsqrt(1.0 + s * s)
        change = along - pltpu.roll(along, 1, 1) + across - pltpu.roll(across, 1, 0)
        work[...] = h + inside[...] * change
        return carry

    lax.fori_loop(0, STEPS, diffuse, 0)

    @pl.when(jnp.logical_not(is_top))
    def _():
        top_copy(1).wait_recv()
        top_own[...] = top_in[...]

    cell_at = lax.broadcasted_iota(jnp.int32, (width, share), 0) * ratio_c
    col = z * share + lax.broadcasted_iota(jnp.int32, (width, share), 1)
    pick = jnp.where((col >= cell_at) & (col < cell_at + ratio_c), 1.0, 0.0)
    spread = jnp.dot(
        top_own[...].reshape(2 * cells, width), pick, precision=HIGH, preferred_element_type=jnp.float32
    )

    for o in OFFSETS:
        pl.when(present(*o))(lambda o=o: rim_copy(*o).wait_send())
    for b, c in surf_offsets:

        def sent(b=b, c=c):
            for copy in surf_copies(b, c):
                copy.wait_send()

        pl.when(surf_present(b, c, False))(sent)

    @pl.when(is_top)
    def _():
        for k in range(1, nz):
            top_copy(k).wait_send()

    most = gathered.at[pl.ds(0, count - 1)]
    pltpu.make_async_copy(most, most, sum_send).wait()
    pltpu.make_async_copy(most, most, sum_recv).wait()

    table = gathered[...].reshape(count, width)
    m0, m1, own, e, ww, waw, baw = [table[:, i : i + 1] for i in range(7)]
    rr = m0.sum(axis=0, keepdims=True)
    bab = m1.sum(axis=0, keepdims=True)
    mean = bab / rr
    off = own - mean
    s2 = (ww + off * (2.0 * e + off * m0)).sum(axis=0, keepdims=True)
    q = (waw + off * (ww + own * e + baw + off * m1)).sum(axis=0, keepdims=True)
    alpha0 = rr / bab
    beta = s2 / (mean * bab)
    alpha1 = s2 / (q - s2 * s2 / bab)
    on_b = alpha0 + alpha1 * (1.0 + beta)
    on_ab = -alpha1 * alpha0
    for f in range(3):
        velocity_ref[f] = on_b * field[f] + on_ab * image[f, 1:-1, 0:cells, 0:width]
    rise = (STEPS * time_step) * (on_b * spread[:cells] + on_ab * spread[cells:])
    rise = jnp.broadcast_to(rise[:, None, :], (cells, ratio_r, share)).reshape(rows, share)
    surface_ref[...] = work[STEPS : STEPS + rows, 0:share] + rise


def local(sizes, body_force, viscosity, topography, kappa):
    depth, cells, width = viscosity.shape
    rows, cols = topography.shape
    nx, ny, nz = sizes
    count = nx * ny * nz
    share = cols // nz
    f32 = jnp.float32
    dma = pltpu.SemaphoreType.DMA
    return pl.pallas_call(
        functools.partial(kernel, sizes),
        out_shape=(
            jax.ShapeDtypeStruct(body_force.shape, f32),
            jax.ShapeDtypeStruct((rows, share), f32),
        ),
        in_specs=[pl.BlockSpec(memory_space=pl.ANY)] * 4,
        out_specs=[pl.BlockSpec(memory_space=pltpu.VMEM)] * 2,
        scratch_shapes=[
            pltpu.VMEM((4, depth, cells, width), f32),
            pltpu.VMEM((cells, width), f32),
            pltpu.VMEM((2, depth, cells, width), f32),
            pltpu.VMEM((2, 4, REACH, cells, width), f32),
            pltpu.VMEM((2, depth, cells, width), f32),
            pltpu.VMEM((2, 2, 2, cells, width), f32),
            pltpu.VMEM((9, 2, cells, width), f32),
            pltpu.VMEM((4, depth + 2 * REACH, 2 * cells, 2 * width), f32),
            pltpu.VMEM((3, depth + 2 * REACH - 2, 2 * cells, 2 * width), f32),
            pltpu.VMEM((rows + 2 * STEPS, cols + 2 * width), f32),
            pltpu.VMEM((rows + 32, cols + 2 * width), kappa.dtype),
            pltpu.VMEM((rows + 2 * STEPS, share + width), f32),
            pltpu.VMEM((rows + 2 * STEPS, share + width), f32),
            pltpu.VMEM((rows + 2 * STEPS, share + width), f32),
            pltpu.VMEM((rows + 2 * STEPS, share + width), f32),
            pltpu.VMEM((1, 1, width), f32),
            pltpu.VMEM((count, 1, width), f32),
            pltpu.VMEM((2, cells, width), f32),
            pltpu.VMEM((2, cells, width), f32),
            dma((4,)),
            dma((27,)),
            dma((27,)),
            dma((2, 9)),
            dma((2, 9)),
            dma,
            dma,
            dma((nz,)),
            dma,
        ],
        compiler_params=pltpu.CompilerParams(
            collective_id=0, has_side_effects=True, vmem_limit_bytes=32 * 1024 * 1024
        ),
    )(body_force, viscosity, topography, kappa)


def solution(mesh):
    sizes = tuple(mesh.shape[axis] for axis in ("gx", "gy", "gz"))
    in_specs = (P(None, "gz", "gx", "gy"), P("gz", "gx", "gy"), P("gx", "gy"), P("gx", "gy"))
    out_specs = (P(None, "gz", "gx", "gy"), P("gx", ("gy", "gz")))
    return jax.shard_map(
        functools.partial(local, sizes), mesh=mesh, in_specs=in_specs, out_specs=out_specs, check_vma=False
    )
```

time: 247 us -> 23.2 us (0.09)
  blocking collectives: 129 us -> 0 us
  starting transfers between devices: 68.4 us -> 0 us
  Pallas kernels: 0 us -> 17.5 us
  other arithmetic: 17.3 us -> 0 us
  waiting for transfers between devices: 13.3 us -> 0 us
  local copies, waits for them, and re-layouts: 12.5 us -> 4.79 us
  between operations: 5.53 us -> 0.65 us
    psum x4 -> x0, blocking collectives: 129 us -> none  [the longest x2 82 us: squares(): return lax.psum(jnp.sum(residual * residual), ('gx', 'gy', 'gz'))]
    ppermute x26 -> x0, starting transfers between devices: 68.4 us -> none  [the longest x13 51.2 us: extended_2(): lax.ppermute(tail, axis, [(i, (i + 1) % count) for i in range(ends)])]
    pallas_call x0 -> x1, Pallas kernels: none -> 17.5 us  [local(): pl.pallas_call(functools.partial(kernel, sizes), out_shape=(jax.ShapeDtyp...]
    ppermute x26 -> x0, waiting for transfers between devices: 13.3 us -> none  [the longest x13 9.47 us: extended_2(): lax.ppermute(head, axis, [((i + 1) % count, i) for i in range(ends)])]
    reduce_sum x4 -> x0, other arithmetic: 6.04 us -> none  [the longest x2 2.88 us: local(): alpha = norm_now / lax.psum(jnp.sum(direction * image), ('gx', 'gy', 'gz'))]
    unnamed x12 -> x10, local copies, waits for them, and re-layouts: 0.04 us -> 4.79 us
    div x16 -> x0, other arithmetic: 4.62 us -> none  [flux(): return conduct * slope / jnp.sqrt(1.0 + slope * slope)]
    reshape x1 -> x0, local copies, waits for them, and re-layouts: 4.57 us -> none  [local(): topography.reshape(row_cells, row_ratio, col_cells, col_ratio)]
  transfers between devices with their start and end apart: 26 -> 0, of which waited for: 7 -> 0; matrix products, arithmetic and copies ran while one was open for 4% -> 0% of each run, Pallas kernels for 0% -> 0%
where the time goes in v1:
time: 23.2 us; the launch traced here: 22.9 us
  Pallas kernels  17.5 us (75%)
  local copies, waits for them, and re-layouts  4.79 us (21%)
  between operations  0.65 us (3%)
    pallas_call x1, Pallas kernels, local(): pl.pallas_call(functools.partial(kernel, sizes), out_shape=(jax.ShapeDtyp...  17.5 us
    unnamed x10, local copies, waits for them, and re-layouts  4.79 us

profile of v1, /device:TPU:0, one launch (start us, length us, event | category | flops | bytes accessed | tf_op | source)
XLA Modules:
  0.0 22.9 jit_solution(4386277738133545563)
XLA Ops:
  0.6 0.0 copy-start
  0.6 0.9 %copy-done = f32[64,1024]{1,0:T(8,128)S(1)} copy-done((f32[64,1024]{1,0:T(8,128)S(1)}, f32[64,1024]{1,0:T(8,128)}, u32[]{:S(2)}) %copy-start) | copy-done | bytes 262168
  1.6 0.0 copy-start.1
  1.6 0.9 %copy-done.1 = bf16[64,1024]{1,0:T(8,128)(2,1)S(1)} copy-done((bf16[64,1024]{1,0:T(8,128)(2,1)S(1)}, bf16[64,1024]{1,0:T(8,128)(2,1)}, u32[]{:S(2)}) %copy-start.1) | copy-done | bytes 131096
  2.5 0.0 copy-start.2
  2.5 0.9 %copy-done.2 = f32[3,8,8,128]{3,2,1,0:T(8,128)S(1)} copy-done((f32[3,8,8,128]{3,2,1,0:T(8,128)S(1)}, f32[3,8,8,128]{3,2,1,0:T(8,128)}, u32[]{:S(2)}) %copy-start.2) | copy-done | bytes 98328
  3.4 0.0 copy-start.3
  3.4 0.8 %copy-done.3 = f32[8,8,128]{2,1,0:T(8,128)S(1)} copy-done((f32[8,8,128]{2,1,0:T(8,128)S(1)}, f32[8,8,128]{2,1,0:T(8,128)}, u32[]{:S(2)}) %copy-start.3) | copy-done | bytes 32792
  4.1 17.5 %shard_map.59 = (f32[3,8,8,128]{3,2,1,0:T(8,128)S(1)}, f32[64,512]{1,0:T(8,128)S(1)}) custom-call(f32[3,8,8,128]{3,2,1,0:T(8,128)S(1)} %copy-done.2, f32[8,8,128]{2,1,0:T(8,128)S(1)} %copy-done.3, f32[64,1024]{1,0:T(8,128)S(1)} %copy-done, bf16[64,1024]{1,0:T(8,128)(2,1)S(1)} %copy-done.1), custom_call_target="tpu_custom_call" | custom-call | tf_op jit(solution)/shard_map/pallas_call | solution.py:432
  21.6 0.6 %copy.8 = f32[3,8,8,128]{3,2,1,0:T(8,128)} copy(f32[3,8,8,128]{3,2,1,0:T(8,128)S(1)} %get-tuple-element.4) | data formatting | bytes 196608
  22.3 0.7 %copy.9 = f32[64,512]{1,0:T(8,128)} copy(f32[64,512]{1,0:T(8,128)S(1)} %get-tuple-element.5) | data formatting | bytes 262144
Async XLA Ops:
  0.6 1.0 %copy-start = (f32[64,1024]{1,0:T(8,128)S(1)}, f32[64,1024]{1,0:T(8,128)}, u32[]{:S(2)}) copy-start(f32[64,1024]{1,0:T(8,128)} %topo_hbm.1) | copy-start | bytes 786436
  1.6 0.9 %copy-start.1 = (bf16[64,1024]{1,0:T(8,128)(2,1)S(1)}, bf16[64,1024]{1,0:T(8,128)(2,1)}, u32[]{:S(2)}) copy-start(bf16[64,1024]{1,0:T(8,128)(2,1)} %kappa_hbm.1) | copy-start | bytes 393220
  2.5 0.9 %copy-start.2 = (f32[3,8,8,128]{3,2,1,0:T(8,128)S(1)}, f32[3,8,8,128]{3,2,1,0:T(8,128)}, u32[]{:S(2)}) copy-start(f32[3,8,8,128]{3,2,1,0:T(8,128)} %force_hbm.1) | copy-start | bytes 294916
  3.4 0.8 %copy-start.3 = (f32[8,8,128]{2,1,0:T(8,128)S(1)}, f32[8,8,128]{2,1,0:T(8,128)}, u32[]{:S(2)}) copy-start(f32[8,8,128]{2,1,0:T(8,128)} %visc_hbm.1) | copy-start | bytes 98308

commit v2 on v1

--- a/solution.py
+++ b/solution.py
@@ -20,7 +20,6 @@
 W_ALL = 6 * W_FACE + 12 * W_EDGE + 8 * W_CORNER
 
 MESH = pl.DeviceIdType.MESH
-HIGH = lax.Precision.HIGHEST
 SIGNS = (-1, 0, 1)
 OFFSETS = [(a, b, c) for a in SIGNS for b in SIGNS for c in SIGNS if (a, b, c) != (0, 0, 0)]
 
@@ -41,6 +40,18 @@
     same = W_FACE * near + W_EDGE * diagonal
     other = W_FACE * u + W_EDGE * near + W_CORNER * diagonal
     return same[1:-1] + other[:-2] + other[2:]
+
+
+def picked(x, choice):
+    parts = []
+    for _ in range(3):
+        part = x.astype(jnp.bfloat16)
+        parts.append(part.astype(jnp.float32))
+        x = x - parts[-1]
+    rows = x.shape[0]
+    stacked = jnp.concatenate(parts, axis=0).astype(jnp.bfloat16)
+    out = jnp.dot(stacked, choice, preferred_element_type=jnp.float32)
+    return out[:rows] + (out[rows : 2 * rows] + out[2 * rows :])
 
 
 def total(x):
@@ -130,7 +141,7 @@
     at = lax.broadcasted_iota(jnp.int32, (cols, width), 0)
     first = lax.broadcasted_iota(jnp.int32, (cols, width), 1) * ratio_c
     pick = jnp.where((at >= first) & (at < first + ratio_c), 1.0, 0.0)
-    load = jnp.dot(by_rows, pick, precision=HIGH, preferred_element_type=jnp.float32) / (ratio_r * ratio_c)
+    load = picked(by_rows, pick.astype(jnp.bfloat16)) * (1.0 / (ratio_r * ratio_c))
     loads[1].wait()
     loads[2].wait()
     field[2, depth - 1] = field[2, depth - 1] + jnp.where(is_top, -load_gain * load, 0.0)
@@ -378,9 +389,7 @@
     cell_at = lax.broadcasted_iota(jnp.int32, (width, share), 0) * ratio_c
     col = z * share + lax.broadcasted_iota(jnp.int32, (width, share), 1)
     pick = jnp.where((col >= cell_at) & (col < cell_at + ratio_c), 1.0, 0.0)
-    spread = jnp.dot(
-        top_own[...].reshape(2 * cells, width), pick, precision=HIGH, preferred_element_type=jnp.float32
-    )
+    spread = picked(top_own[...].reshape(2 * cells, width), pick.astype(jnp.bfloat16))
 
     for o in OFFSETS:
         pl.when(present(*o))(lambda o=o: rim_copy(*o).wait_send())
@@ -421,6 +430,17 @@
     surface_ref[...] = work[STEPS : STEPS + rows, 0:share] + rise
 
 
+def put(velocity_in, surface_in, velocity_out, surface_out, sems):
+    copies = [
+        pltpu.make_async_copy(velocity_in, velocity_out, sems.at[0]),
+        pltpu.make_async_copy(surface_in, surface_out, sems.at[1]),
+    ]
+    for copy in copies:
+        copy.start()
+    for copy in copies:
+        copy.wait()
+
+
 def local(sizes, body_force, viscosity, topography, kappa):
     depth, cells, width = viscosity.shape
     rows, cols = topography.shape
@@ -429,13 +449,13 @@
     share = cols // nz
     f32 = jnp.float32
     dma = pltpu.SemaphoreType.DMA
-    return pl.pallas_call(
+    made = pl.pallas_call(
         functools.partial(kernel, sizes),
         out_shape=(
             jax.ShapeDtypeStruct(body_force.shape, f32),
             jax.ShapeDtypeStruct((rows, share), f32),
         ),
-        in_specs=[pl.BlockSpec(memory_space=pl.ANY)] * 4,
+        in_specs=[pl.BlockSpec(memory_space=pltpu.HBM)] * 4,
         out_specs=[pl.BlockSpec(memory_space=pltpu.VMEM)] * 2,
         scratch_shapes=[
             pltpu.VMEM((4, depth, cells, width), f32),
@@ -470,7 +490,14 @@
         compiler_params=pltpu.CompilerParams(
             collective_id=0, has_side_effects=True, vmem_limit_bytes=32 * 1024 * 1024
         ),
-    )(body_force, viscosity, topography, kappa)
+    )(*[pltpu.with_memory_space_constraint(one, pltpu.HBM) for one in (body_force, viscosity, topography, kappa)])
+    return pl.pallas_call(
+        put,
+        out_shape=tuple(jax.ShapeDtypeStruct(one.shape, one.dtype) for one in made),
+        in_specs=[pl.BlockSpec(memory_space=pltpu.VMEM)] * 2,
+        out_specs=[pl.BlockSpec(memory_space=pltpu.HBM)] * 2,
+        scratch_shapes=[dma((2,))],
+    )(*made)
 
 
 def solution(mesh):

time: 23.2 us -> 21 us (0.905)
  local copies, waits for them, and re-layouts: 4.79 us -> 1.28 us
  Pallas kernels: 17.5 us -> 18.9 us
    unnamed x10 -> x4, local copies, waits for them, and re-layouts: 4.79 us -> 1.28 us
    pallas_call x0 -> x1, Pallas kernels: none -> 1.65 us  [local(): pl.pallas_call(put, out_shape=tuple((jax.ShapeDtypeStruct(one.shape, one....]
where the time goes in v2:
time: 21 us; the launch traced here: 20.9 us
  Pallas kernels  18.9 us (90%)
  local copies, waits for them, and re-layouts  1.28 us (6%)
  between operations  0.65 us (3%)
    pallas_call x1, Pallas kernels, local(): pl.pallas_call(functools.partial(kernel, sizes), out_shape=(jax.ShapeDtyp...  17.3 us
    pallas_call x1, Pallas kernels, local(): pl.pallas_call(put, out_shape=tuple((jax.ShapeDtypeStruct(one.shape, one....  1.65 us
    unnamed x4, local copies, waits for them, and re-layouts  1.28 us

profile of v2, /device:TPU:0, one launch (start us, length us, event | category | flops | bytes accessed | tf_op | source)
XLA Modules:
  0.0 20.9 jit_solution(9438204020255313393)
XLA Ops:
  0.6 17.3 %shard_map.59 = (f32[3,8,8,128]{3,2,1,0:T(8,128)S(1)}, f32[64,512]{1,0:T(8,128)S(1)}) custom-call(f32[3,8,8,128]{3,2,1,0:T(8,128)} %force_hbm.1, f32[8,8,128]{2,1,0:T(8,128)} %visc_hbm.1, f32[64,1024]{1,0:T(8,128)} %topo_hbm.1, bf16[64,1024]{1,0:T(8,128)(2,1)} %kappa_hbm.1), custom_call_target="tpu_custom_call" | custom-call | tf_op jit(solution)/shard_map/pallas_call | solution.py:452
  17.9 0.0 copy-start
  17.9 0.6 %copy-done = f32[64,512]{1,0:T(8,128)} copy-done((f32[64,512]{1,0:T(8,128)}, f32[64,512]{1,0:T(8,128)S(1)}, u32[]{:S(2)}) %copy-start) | copy-done | bytes 131096
  18.6 0.0 copy-start.1
  18.6 0.6 %copy-done.1 = f32[3,8,8,128]{3,2,1,0:T(8,128)} copy-done((f32[3,8,8,128]{3,2,1,0:T(8,128)}, f32[3,8,8,128]{3,2,1,0:T(8,128)S(1)}, u32[]{:S(2)}) %copy-start.1) | copy-done | bytes 98328
  19.2 1.7 %shard_map.60 = (f32[3,8,8,128]{3,2,1,0:T(8,128)}, f32[64,512]{1,0:T(8,128)}) custom-call(f32[3,8,8,128]{3,2,1,0:T(8,128)} %copy-done.1, f32[64,512]{1,0:T(8,128)} %copy-done), custom_call_target="tpu_custom_call" | custom-call | tf_op jit(solution)/shard_map/pallas_call | solution.py:494
Async XLA Ops:
  17.9 0.6 %copy-start = (f32[64,512]{1,0:T(8,128)}, f32[64,512]{1,0:T(8,128)S(1)}, u32[]{:S(2)}) copy-start(f32[64,512]{1,0:T(8,128)S(1)} %get-tuple-element.5.surface_in) | copy-start | bytes 393220
  18.6 0.6 %copy-start.1 = (f32[3,8,8,128]{3,2,1,0:T(8,128)}, f32[3,8,8,128]{3,2,1,0:T(8,128)S(1)}, u32[]{:S(2)}) copy-start(f32[3,8,8,128]{3,2,1,0:T(8,128)S(1)} %get-tuple-element.4.velocity_in) | copy-start | bytes 294916

commit v3 on v2

--- a/solution.py
+++ b/solution.py
@@ -9,6 +9,7 @@
 
 STEPS = 8
 REACH = 2
+EARLY = 4
 
 drag = 1.0
 time_step = 1.0
@@ -35,11 +36,11 @@
 def weighted(u):
     rows, lanes = u.shape[1:]
     beside = pltpu.roll(u, 1, 2) + pltpu.roll(u, lanes - 1, 2)
-    near = beside + pltpu.roll(u, 1, 1) + pltpu.roll(u, rows - 1, 1)
-    diagonal = pltpu.roll(beside, 1, 1) + pltpu.roll(beside, rows - 1, 1)
-    same = W_FACE * near + W_EDGE * diagonal
-    other = W_FACE * u + W_EDGE * near + W_CORNER * diagonal
-    return same[1:-1] + other[:-2] + other[2:]
+    near = W_FACE * u + W_EDGE * beside
+    far = W_EDGE * u + W_CORNER * beside
+    level = W_FACE * beside[1:-1] + (near[:-2] + near[2:])
+    next_row = near[1:-1] + (far[:-2] + far[2:])
+    return level + (pltpu.roll(next_row, 1, 1) + pltpu.roll(next_row, rows - 1, 1))
 
 
 def picked(x, choice):
@@ -132,16 +133,71 @@
     conduct[krow : krow + rows, width + cols :] = jnp.zeros((rows, width), conduct.dtype)
 
     barrier = pltpu.get_barrier_semaphore()
-    for a, b, c in others:
+    for a, b, c in reversed(others):
         pl.semaphore_signal(barrier, inc=1, device_id=(xs[a], ys[b], zs[c]), device_id_type=MESH)
 
-    loads[0].wait()
     ratio_r, ratio_c = rows // cells, cols // width
-    by_rows = height[STEPS : STEPS + rows, width : width + cols].reshape(cells, ratio_r, cols).sum(axis=1)
     at = lax.broadcasted_iota(jnp.int32, (cols, width), 0)
     first = lax.broadcasted_iota(jnp.int32, (cols, width), 1) * ratio_c
-    pick = jnp.where((at >= first) & (at < first + ratio_c), 1.0, 0.0)
-    load = picked(by_rows, pick.astype(jnp.bfloat16)) * (1.0 / (ratio_r * ratio_c))
+    pick = jnp.where((at >= first) & (at < first + ratio_c), 1.0, 0.0).astype(jnp.bfloat16)
+
+    pl.semaphore_wait(barrier, count - 1)
+
+    def present(a, b, c):
+        yes = None
+        for sign, at_, size in ((a, z, nz), (b, x, nx), (c, y, ny)):
+            if sign:
+                one = at_ > 0 if sign < 0 else at_ < size - 1
+                yes = one if yes is None else jnp.logical_and(yes, one)
+        return yes
+
+    surf_offsets = [(b, c) for b in SIGNS for c in SIGNS if (b, c) != (0, 0)]
+
+    def surf_present(b, c, receiving):
+        yes = present(0, b, c)
+        toward = -c if receiving else c
+        if toward > 0:
+            yes = jnp.logical_and(yes, z == 0)
+        if toward < 0:
+            yes = jnp.logical_and(yes, z == nz - 1)
+        return yes
+
+    def surf_copies(b, c):
+        def spans(sign, size, halo, lead):
+            if sign == 0:
+                return slice(0, size), slice(lead, lead + size)
+            if sign > 0:
+                return slice(size - halo, size), slice(0, halo)
+            return slice(0, halo), slice(lead + size, lead + size + halo)
+
+        cs, cd = spans(c, cols, width, width)
+        n = (b + 1) * 3 + (c + 1)
+        m = (1 - b) * 3 + (1 - c)
+        made = []
+        for i, (src, dst, halo) in enumerate(((topo_hbm, height, STEPS), (kappa_hbm, conduct, krow))):
+            rs, rd = spans(b, rows, halo, halo)
+            made.append(
+                pltpu.make_async_remote_copy(
+                    src_ref=src.at[rs, cs],
+                    dst_ref=dst.at[rd, cd],
+                    send_sem=surf_send.at[i, n],
+                    recv_sem=surf_recv.at[i, m],
+                    device_id=(x + b, y + c, z),
+                    device_id_type=MESH,
+                )
+            )
+        return made
+
+    def surf_start(b, c):
+        for copy in surf_copies(b, c):
+            copy.start()
+
+    for o in surf_offsets:
+        pl.when(surf_present(*o, False))(lambda o=o: surf_start(*o))
+
+    loads[0].wait()
+    by_rows = height[STEPS : STEPS + rows, width : width + cols].reshape(cells, ratio_r, cols).sum(axis=1)
+    load = picked(by_rows, pick) * (1.0 / (ratio_r * ratio_c))
     loads[1].wait()
     loads[2].wait()
     field[2, depth - 1] = field[2, depth - 1] + jnp.where(is_top, -load_gain * load, 0.0)
@@ -166,14 +222,6 @@
         row_pack[0, t] = up_pack[t]
         row_pack[1, t] = down_pack[t]
 
-    def present(a, b, c):
-        yes = None
-        for sign, at_, size in ((a, z, nz), (b, x, nx), (c, y, ny)):
-            if sign:
-                one = at_ > 0 if sign < 0 else at_ < size - 1
-                yes = one if yes is None else jnp.logical_and(yes, one)
-        return yes
-
     def rim_copy(a, b, c):
         span = slice(depth - 2, depth) if a > 0 else slice(0, 2)
         if c != 0:
@@ -193,53 +241,50 @@
             device_id_type=MESH,
         )
 
-    pl.semaphore_wait(barrier, count - 1)
     for o in OFFSETS:
         pl.when(present(*o))(lambda o=o: rim_copy(*o).start())
 
-    surf_offsets = [(b, c) for b in SIGNS for c in SIGNS if (b, c) != (0, 0)]
-
-    def surf_present(b, c, receiving):
-        yes = present(0, b, c)
-        toward = -c if receiving else c
-        if toward > 0:
-            yes = jnp.logical_and(yes, z == 0)
-        if toward < 0:
-            yes = jnp.logical_and(yes, z == nz - 1)
-        return yes
-
-    def surf_copies(b, c):
-        def spans(sign, size, halo, lead):
-            if sign == 0:
-                return slice(0, size), slice(lead, lead + size)
-            if sign > 0:
-                return slice(size - halo, size), slice(0, halo)
-            return slice(0, halo), slice(lead + size, lead + size + halo)
-
-        cs, cd = spans(c, cols, width, width)
-        n = (b + 1) * 3 + (c + 1)
-        m = (1 - b) * 3 + (1 - c)
-        made = []
-        for i, (src, dst, halo) in enumerate(((topo_hbm, height, STEPS), (kappa_hbm, conduct, krow))):
-            rs, rd = spans(b, rows, halo, halo)
-            made.append(
-                pltpu.make_async_remote_copy(
-                    src_ref=src.at[rs, cs],
-                    dst_ref=dst.at[rd, cd],
-                    send_sem=surf_send.at[i, n],
-                    recv_sem=surf_recv.at[i, m],
-                    device_id=(x + b, y + c, z),
-                    device_id_type=MESH,
-                )
-            )
-        return made
-
-    def surf_start(b, c):
-        for copy in surf_copies(b, c):
-            copy.start()
-
-    for o in surf_offsets:
-        pl.when(surf_present(*o, False))(lambda o=o: surf_start(*o))
+    for b, c in surf_offsets:
+
+        def arrived(b=b, c=c):
+            for copy in surf_copies(-b, -c):
+                copy.wait_recv()
+
+        pl.when(surf_present(b, c, True))(arrived)
+    loads[3].wait()
+    start = pl.multiple_of(z * share, share)
+    tall = rows + 2 * STEPS
+    left_half = lax.broadcasted_iota(jnp.int32, (1, width), 1) < width // 2
+
+    def joined_window(ref):
+        wide = ref[:, pl.ds(start, share + 2 * width)].astype(jnp.float32)
+        rim = jnp.where(left_half, wide[:, width + share :], wide[:, :width])
+        return jnp.concatenate([wide[:, width : width + share], rim], axis=1)
+
+    work[...] = joined_window(height)
+    k = joined_window(conduct)[krow - STEPS : krow + rows + STEPS]
+    span = share + width
+    face_right[...] = 0.5 * (k + pltpu.roll(k, span - 1, 1))
+    face_down[...] = 0.5 * (k + pltpu.roll(k, tall - 1, 0))
+    row_at = x * rows - STEPS + lax.broadcasted_iota(jnp.int32, (tall, span), 0)
+    lane_at = lax.broadcasted_iota(jnp.int32, (tall, span), 1)
+    lane_at = jnp.where(lane_at >= span - width // 2, lane_at - span, lane_at)
+    col_at = y * cols + z * share + lane_at
+    inside[...] = jnp.where(
+        (row_at >= 0) & (row_at < rows * nx) & (col_at >= 0) & (col_at < cols * ny), time_step, 0.0
+    )
+
+    def diffuse(_, carry):
+        h = work[...]
+        s = pltpu.roll(h, span - 1, 1) - h
+        along = face_right[...] * s * lax.rsqrt(1.0 + s * s)
+        s = pltpu.roll(h, tall - 1, 0) - h
+        across = face_down[...] * s * lax.rsqrt(1.0 + s * s)
+        change = along - pltpu.roll(along, 1, 1) + across - pltpu.roll(across, 1, 0)
+        work[...] = h + inside[...] * change
+        return carry
+
+    lax.fori_loop(0, EARLY, diffuse, 0)
 
     for a, b, c in OFFSETS:
         pl.when(present(a, b, c))(lambda o=(-a, -b, -c): rim_copy(*o).wait_recv())
@@ -339,47 +384,7 @@
         for k in range(1, nz):
             top_copy(k).start()
 
-    for b, c in surf_offsets:
-
-        def arrived(b=b, c=c):
-            for copy in surf_copies(-b, -c):
-                copy.wait_recv()
-
-        pl.when(surf_present(b, c, True))(arrived)
-    loads[3].wait()
-    start = pl.multiple_of(z * share, share)
-    tall = rows + 2 * STEPS
-    left_half = lax.broadcasted_iota(jnp.int32, (1, width), 1) < width // 2
-
-    def joined_window(ref):
-        wide = ref[:, pl.ds(start, share + 2 * width)].astype(jnp.float32)
-        rim = jnp.where(left_half, wide[:, width + share :], wide[:, :width])
-        return jnp.concatenate([wide[:, width : width + share], rim], axis=1)
-
-    work[...] = joined_window(height)
-    k = joined_window(conduct)[krow - STEPS : krow + rows + STEPS]
-    span = share + width
-    face_right[...] = 0.5 * (k + pltpu.roll(k, span - 1, 1))
-    face_down[...] = 0.5 * (k + pltpu.roll(k, tall - 1, 0))
-    row_at = x * rows - STEPS + lax.broadcasted_iota(jnp.int32, (tall, span), 0)
-    lane_at = lax.broadcasted_iota(jnp.int32, (tall, span), 1)
-    lane_at = jnp.where(lane_at >= span - width // 2, lane_at - span, lane_at)
-    col_at = y * cols + z * share + lane_at
-    inside[...] = jnp.where(
-        (row_at >= 0) & (row_at < rows * nx) & (col_at >= 0) & (col_at < cols * ny), time_step, 0.0
-    )
-
-    def diffuse(_, carry):
-        h = work[...]
-        s = pltpu.roll(h, span - 1, 1) - h
-        along = face_right[...] * s * lax.rsqrt(1.0 + s * s)
-        s = pltpu.roll(h, tall - 1, 0) - h
-        across = face_down[...] * s * lax.rsqrt(1.0 + s * s)
-        change = along - pltpu.roll(along, 1, 1) + across - pltpu.roll(across, 1, 0)
-        work[...] = h + inside[...] * change
-        return carry
-
-    lax.fori_loop(0, STEPS, diffuse, 0)
+    lax.fori_loop(EARLY, STEPS, diffuse, 0)
 
     @pl.when(jnp.logical_not(is_top))
     def _():
@@ -430,17 +435,6 @@
     surface_ref[...] = work[STEPS : STEPS + rows, 0:share] + rise
 
 
-def put(velocity_in, surface_in, velocity_out, surface_out, sems):
-    copies = [
-        pltpu.make_async_copy(velocity_in, velocity_out, sems.at[0]),
-        pltpu.make_async_copy(surface_in, surface_out, sems.at[1]),
-    ]
-    for copy in copies:
-        copy.start()
-    for copy in copies:
-        copy.wait()
-
-
 def local(sizes, body_force, viscosity, topography, kappa):
     depth, cells, width = viscosity.shape
     rows, cols = topography.shape
@@ -449,7 +443,7 @@
     share = cols // nz
     f32 = jnp.float32
     dma = pltpu.SemaphoreType.DMA
-    made = pl.pallas_call(
+    return pl.pallas_call(
         functools.partial(kernel, sizes),
         out_shape=(
             jax.ShapeDtypeStruct(body_force.shape, f32),
@@ -491,13 +485,6 @@
             collective_id=0, has_side_effects=True, vmem_limit_bytes=32 * 1024 * 1024
         ),
     )(*[pltpu.with_memory_space_constraint(one, pltpu.HBM) for one in (body_force, viscosity, topography, kappa)])
-    return pl.pallas_call(
-        put,
-        out_shape=tuple(jax.ShapeDtypeStruct(one.shape, one.dtype) for one in made),
-        in_specs=[pl.BlockSpec(memory_space=pltpu.VMEM)] * 2,
-        out_specs=[pl.BlockSpec(memory_space=pltpu.HBM)] * 2,
-        scratch_shapes=[dma((2,))],
-    )(*made)
 
 
 def solution(mesh):

time: 21 us -> 20.6 us (0.981)
  Pallas kernels: 18.9 us -> 18.5 us
    pallas_call x1 -> x0, Pallas kernels: 1.65 us -> none  [local(): pl.pallas_call(put, out_shape=tuple((jax.ShapeDtypeStruct(one.shape, one....]
    pallas_call x1, Pallas kernels: 17.3 us -> 18.5 us  [local(): pl.pallas_call(functools.partial(kernel, sizes), out_shape=(jax.ShapeDtyp...]
    unnamed x4 -> x2, local copies, waits for them, and re-layouts: 1.28 us -> 1.3 us
where the time goes in v3:
time: 20.6 us; the launch traced here: 20.4 us
  Pallas kernels  18.5 us (90%)
  local copies, waits for them, and re-layouts  1.3 us (6%)
  between operations  0.64 us (3%)
    pallas_call x1, Pallas kernels, local(): pl.pallas_call(functools.partial(kernel, sizes), out_shape=(jax.ShapeDtyp...  18.5 us
    unnamed x2, local copies, waits for them, and re-layouts  1.3 us

profile of v3, /device:TPU:0, one launch (start us, length us, event | category | flops | bytes accessed | tf_op | source)
XLA Modules:
  0.0 20.4 jit_solution(10435471850893223799)
XLA Ops:
  0.6 18.5 %shard_map.59 = (f32[3,8,8,128]{3,2,1,0:T(8,128)S(1)}, f32[64,512]{1,0:T(8,128)S(1)}) custom-call(f32[3,8,8,128]{3,2,1,0:T(8,128)} %force_hbm.1, f32[8,8,128]{2,1,0:T(8,128)} %visc_hbm.1, f32[64,1024]{1,0:T(8,128)} %topo_hbm.1, bf16[64,1024]{1,0:T(8,128)(2,1)} %kappa_hbm.1), custom_call_target="tpu_custom_call" | custom-call | tf_op jit(solution)/shard_map/pallas_call | solution.py:446
  19.1 0.6 %copy.8 = f32[3,8,8,128]{3,2,1,0:T(8,128)} copy(f32[3,8,8,128]{3,2,1,0:T(8,128)S(1)} %get-tuple-element.4) | data formatting | bytes 196608
  19.8 0.7 %copy.9 = f32[64,512]{1,0:T(8,128)} copy(f32[64,512]{1,0:T(8,128)S(1)} %get-tuple-element.5) | data formatting | bytes 262144

commit v4 on v2

--- a/solution.py
+++ b/solution.py
@@ -35,11 +35,11 @@
 def weighted(u):
     rows, lanes = u.shape[1:]
     beside = pltpu.roll(u, 1, 2) + pltpu.roll(u, lanes - 1, 2)
-    near = beside + pltpu.roll(u, 1, 1) + pltpu.roll(u, rows - 1, 1)
-    diagonal = pltpu.roll(beside, 1, 1) + pltpu.roll(beside, rows - 1, 1)
-    same = W_FACE * near + W_EDGE * diagonal
-    other = W_FACE * u + W_EDGE * near + W_CORNER * diagonal
-    return same[1:-1] + other[:-2] + other[2:]
+    near = W_FACE * u + W_EDGE * beside
+    far = W_EDGE * u + W_CORNER * beside
+    level = W_FACE * beside[1:-1] + (near[:-2] + near[2:])
+    next_row = near[1:-1] + (far[:-2] + far[2:])
+    return level + (pltpu.roll(next_row, 1, 1) + pltpu.roll(next_row, rows - 1, 1))
 
 
 def picked(x, choice):
@@ -132,16 +132,25 @@
     conduct[krow : krow + rows, width + cols :] = jnp.zeros((rows, width), conduct.dtype)
 
     barrier = pltpu.get_barrier_semaphore()
-    for a, b, c in others:
+    for a, b, c in reversed(others):
         pl.semaphore_signal(barrier, inc=1, device_id=(xs[a], ys[b], zs[c]), device_id_type=MESH)
 
-    loads[0].wait()
     ratio_r, ratio_c = rows // cells, cols // width
-    by_rows = height[STEPS : STEPS + rows, width : width + cols].reshape(cells, ratio_r, cols).sum(axis=1)
     at = lax.broadcasted_iota(jnp.int32, (cols, width), 0)
     first = lax.broadcasted_iota(jnp.int32, (cols, width), 1) * ratio_c
-    pick = jnp.where((at >= first) & (at < first + ratio_c), 1.0, 0.0)
-    load = picked(by_rows, pick.astype(jnp.bfloat16)) * (1.0 / (ratio_r * ratio_c))
+    pick = jnp.where((at >= first) & (at < first + ratio_c), 1.0, 0.0).astype(jnp.bfloat16)
+
+    def present(a, b, c):
+        yes = None
+        for sign, at_, size in ((a, z, nz), (b, x, nx), (c, y, ny)):
+            if sign:
+                one = at_ > 0 if sign < 0 else at_ < size - 1
+                yes = one if yes is None else jnp.logical_and(yes, one)
+        return yes
+
+    loads[0].wait()
+    by_rows = height[STEPS : STEPS + rows, width : width + cols].reshape(cells, ratio_r, cols).sum(axis=1)
+    load = picked(by_rows, pick) * (1.0 / (ratio_r * ratio_c))
     loads[1].wait()
     loads[2].wait()
     field[2, depth - 1] = field[2, depth - 1] + jnp.where(is_top, -load_gain * load, 0.0)
@@ -165,14 +174,6 @@
     for t in range(depth):
         row_pack[0, t] = up_pack[t]
         row_pack[1, t] = down_pack[t]
-
-    def present(a, b, c):
-        yes = None
-        for sign, at_, size in ((a, z, nz), (b, x, nx), (c, y, ny)):
-            if sign:
-                one = at_ > 0 if sign < 0 else at_ < size - 1
-                yes = one if yes is None else jnp.logical_and(yes, one)
-        return yes
 
     def rim_copy(a, b, c):
         span = slice(depth - 2, depth) if a > 0 else slice(0, 2)
@@ -430,17 +431,6 @@
     surface_ref[...] = work[STEPS : STEPS + rows, 0:share] + rise
 
 
-def put(velocity_in, surface_in, velocity_out, surface_out, sems):
-    copies = [
-        pltpu.make_async_copy(velocity_in, velocity_out, sems.at[0]),
-        pltpu.make_async_copy(surface_in, surface_out, sems.at[1]),
-    ]
-    for copy in copies:
-        copy.start()
-    for copy in copies:
-        copy.wait()
-
-
 def local(sizes, body_force, viscosity, topography, kappa):
     depth, cells, width = viscosity.shape
     rows, cols = topography.shape
@@ -449,7 +439,7 @@
     share = cols // nz
     f32 = jnp.float32
     dma = pltpu.SemaphoreType.DMA
-    made = pl.pallas_call(
+    return pl.pallas_call(
         functools.partial(kernel, sizes),
         out_shape=(
             jax.ShapeDtypeStruct(body_force.shape, f32),
@@ -491,13 +481,6 @@
             collective_id=0, has_side_effects=True, vmem_limit_bytes=32 * 1024 * 1024
         ),
     )(*[pltpu.with_memory_space_constraint(one, pltpu.HBM) for one in (body_force, viscosity, topography, kappa)])
-    return pl.pallas_call(
-        put,
-        out_shape=tuple(jax.ShapeDtypeStruct(one.shape, one.dtype) for one in made),
-        in_specs=[pl.BlockSpec(memory_space=pltpu.VMEM)] * 2,
-        out_specs=[pl.BlockSpec(memory_space=pltpu.HBM)] * 2,
-        scratch_shapes=[dma((2,))],
-    )(*made)
 
 
 def solution(mesh):

time: 21 us -> 19.3 us (0.919)
  Pallas kernels: 18.9 us -> 17.2 us
    pallas_call x1 -> x0, Pallas kernels: 1.65 us -> none  [local(): pl.pallas_call(put, out_shape=tuple((jax.ShapeDtypeStruct(one.shape, one....]
    unnamed x4 -> x2, local copies, waits for them, and re-layouts: 1.28 us -> 1.3 us
where the time goes in v4:
time: 19.3 us; the launch traced here: 19.1 us
  Pallas kernels  17.2 us (89%)
  local copies, waits for them, and re-layouts  1.3 us (7%)
  between operations  0.64 us (3%)
    pallas_call x1, Pallas kernels, local(): pl.pallas_call(functools.partial(kernel, sizes), out_shape=(jax.ShapeDtyp...  17.2 us
    unnamed x2, local copies, waits for them, and re-layouts  1.3 us

profile of v4, /device:TPU:0, one launch (start us, length us, event | category | flops | bytes accessed | tf_op | source)
XLA Modules:
  0.0 19.1 jit_solution(913806359948488017)
XLA Ops:
  0.6 17.2 %shard_map.59 = (f32[3,8,8,128]{3,2,1,0:T(8,128)S(1)}, f32[64,512]{1,0:T(8,128)S(1)}) custom-call(f32[3,8,8,128]{3,2,1,0:T(8,128)} %force_hbm.1, f32[8,8,128]{2,1,0:T(8,128)} %visc_hbm.1, f32[64,1024]{1,0:T(8,128)} %topo_hbm.1, bf16[64,1024]{1,0:T(8,128)(2,1)} %kappa_hbm.1), custom_call_target="tpu_custom_call" | custom-call | tf_op jit(solution)/shard_map/pallas_call | solution.py:442
  17.8 0.6 %copy.8 = f32[3,8,8,128]{3,2,1,0:T(8,128)} copy(f32[3,8,8,128]{3,2,1,0:T(8,128)S(1)} %get-tuple-element.4) | data formatting | bytes 196608
  18.5 0.7 %copy.9 = f32[64,512]{1,0:T(8,128)} copy(f32[64,512]{1,0:T(8,128)S(1)} %get-tuple-element.5) | data formatting | bytes 262144

commit v5 on v4

--- a/solution.py
+++ b/solution.py
@@ -9,6 +9,7 @@
 
 STEPS = 8
 REACH = 2
+EARLY = 3
 
 drag = 1.0
 time_step = 1.0
@@ -21,7 +22,10 @@
 
 MESH = pl.DeviceIdType.MESH
 SIGNS = (-1, 0, 1)
-OFFSETS = [(a, b, c) for a in SIGNS for b in SIGNS for c in SIGNS if (a, b, c) != (0, 0, 0)]
+OFFSETS = sorted(
+    [(a, b, c) for a in SIGNS for b in SIGNS for c in SIGNS if (a, b, c) != (0, 0, 0)],
+    key=lambda o: (abs(o[0]) + abs(o[1]) + abs(o[2]), abs(o[2])),
+)
 
 
 def side(sign):
@@ -107,8 +111,6 @@
     xs = [lax.rem(x + k, nx) for k in range(nx)]
     ys = [lax.rem(y + k, ny) for k in range(ny)]
     zs = [lax.rem(z + k, nz) for k in range(nz)]
-    others = [(a, b, c) for a in range(nx) for b in range(ny) for c in range(nz)][1:]
-    others.sort(key=lambda o: -(min(o[0], nx - o[0]) + min(o[1], ny - o[1]) + min(o[2], nz - o[2])))
     is_top = z == nz - 1
 
     loads = [
@@ -132,8 +134,24 @@
     conduct[krow : krow + rows, width + cols :] = jnp.zeros((rows, width), conduct.dtype)
 
     barrier = pltpu.get_barrier_semaphore()
-    for a, b, c in reversed(others):
-        pl.semaphore_signal(barrier, inc=1, device_id=(xs[a], ys[b], zs[c]), device_id_type=MESH)
+    plane = nx * nz
+    in_plane = [(a, c) for a in range(nx) for c in range(nz)]
+
+    def greet(a, at_y, c):
+        pl.semaphore_signal(barrier, inc=1, device_id=(xs[a], at_y, zs[c]), device_id_type=MESH)
+
+    def greet_plane(at_y):
+        for a, c in in_plane:
+            greet(a, at_y, c)
+
+    for a, c in in_plane[1:]:
+        greet(a, y, c)
+    pl.when(y > 0)(lambda: greet_plane(y - 1))
+    pl.when(y < ny - 1)(lambda: greet_plane(y + 1))
+    for k in range(ny):
+        pl.when(jnp.logical_or(y - k > 1, k - y > 1))(lambda k=k: greet(0, k, 0))
+    beside_y = jnp.where(y > 0, 1, 0) + jnp.where(y < ny - 1, 1, 0)
+    greeted = plane + ny - 2 + (plane - 1) * beside_y
 
     ratio_r, ratio_c = rows // cells, cols // width
     at = lax.broadcasted_iota(jnp.int32, (cols, width), 0)
@@ -194,7 +212,7 @@
             device_id_type=MESH,
         )
 
-    pl.semaphore_wait(barrier, count - 1)
+    pl.semaphore_wait(barrier, greeted)
     for o in OFFSETS:
         pl.when(present(*o))(lambda o=o: rim_copy(*o).start())
 
@@ -311,17 +329,18 @@
     for i, number in enumerate(numbers):
         line = jnp.where(spot == i, number, line)
     row_out[0] = line
-    me = (x * ny + y) * nz + z
+    first_of_plane = y * plane
+    me = first_of_plane + x * nz + z
     gathered[me] = line
     top_own[0] = field[2, depth - 1]
     top_own[1] = image[2, depth, 0:cells, 0:width]
-    for a, b, c in others:
+    for a, c in in_plane[1:]:
         pltpu.make_async_remote_copy(
             src_ref=row_out.at[0],
             dst_ref=gathered.at[me],
-            send_sem=sum_send,
-            recv_sem=sum_recv,
-            device_id=(xs[a], ys[b], zs[c]),
+            send_sem=sum_send.at[0],
+            recv_sem=sum_recv.at[0],
+            device_id=(xs[a], y, zs[c]),
             device_id_type=MESH,
         ).start()
 
@@ -380,7 +399,22 @@
         work[...] = h + inside[...] * change
         return carry
 
-    lax.fori_loop(0, STEPS, diffuse, 0)
+    lax.fori_loop(0, EARLY, diffuse, 0)
+
+    most = gathered.at[pl.ds(0, plane - 1)]
+    pltpu.make_async_copy(most, most, sum_recv.at[0]).wait()
+    whole_plane = gathered.at[pl.ds(first_of_plane, plane)]
+    for k in range(1, ny):
+        pltpu.make_async_remote_copy(
+            src_ref=whole_plane,
+            dst_ref=whole_plane,
+            send_sem=sum_send.at[1],
+            recv_sem=sum_recv.at[1],
+            device_id=(x, ys[k], z),
+            device_id_type=MESH,
+        ).start()
+
+    lax.fori_loop(EARLY, STEPS, diffuse, 0)
 
     @pl.when(jnp.logical_not(is_top))
     def _():
@@ -407,9 +441,10 @@
         for k in range(1, nz):
             top_copy(k).wait_send()
 
-    most = gathered.at[pl.ds(0, count - 1)]
-    pltpu.make_async_copy(most, most, sum_send).wait()
-    pltpu.make_async_copy(most, most, sum_recv).wait()
+    rest = gathered.at[pl.ds(0, plane * (ny - 1))]
+    pltpu.make_async_copy(most, most, sum_send.at[0]).wait()
+    pltpu.make_async_copy(rest, rest, sum_send.at[1]).wait()
+    pltpu.make_async_copy(rest, rest, sum_recv.at[1]).wait()
 
     table = gathered[...].reshape(count, width)
     m0, m1, own, e, ww, waw, baw = [table[:, i : i + 1] for i in range(7)]
@@ -472,8 +507,8 @@
             dma((27,)),
             dma((2, 9)),
             dma((2, 9)),
-            dma,
-            dma,
+            dma((2,)),
+            dma((2,)),
             dma((nz,)),
             dma,
         ],

time: 19.3 us -> 21.3 us (1.10)
  Pallas kernels: 17.2 us -> 19.2 us
    pallas_call x1, Pallas kernels: 17.2 us -> 19.2 us  [local(): pl.pallas_call(functools.partial(kernel, sizes), out_shape=(jax.ShapeDtyp...]
where the time goes in v5:
time: 21.3 us; the launch traced here: 21.2 us
  Pallas kernels  19.2 us (90%)
  local copies, waits for them, and re-layouts  1.3 us (6%)
  between operations  0.64 us (3%)
    pallas_call x1, Pallas kernels, local(): pl.pallas_call(functools.partial(kernel, sizes), out_shape=(jax.ShapeDtyp...  19.2 us
    unnamed x2, local copies, waits for them, and re-layouts  1.3 us

profile of v5, /device:TPU:0, one launch (start us, length us, event | category | flops | bytes accessed | tf_op | source)
XLA Modules:
  0.0 21.2 jit_solution(7161780013691844210)
XLA Ops:
  0.6 19.2 %shard_map.59 = (f32[3,8,8,128]{3,2,1,0:T(8,128)S(1)}, f32[64,512]{1,0:T(8,128)S(1)}) custom-call(f32[3,8,8,128]{3,2,1,0:T(8,128)} %force_hbm.1, f32[8,8,128]{2,1,0:T(8,128)} %visc_hbm.1, f32[64,1024]{1,0:T(8,128)} %topo_hbm.1, bf16[64,1024]{1,0:T(8,128)(2,1)} %kappa_hbm.1), custom_call_target="tpu_custom_call" | custom-call | tf_op jit(solution)/shard_map/pallas_call | solution.py:477
  19.9 0.6 %copy.8 = f32[3,8,8,128]{3,2,1,0:T(8,128)} copy(f32[3,8,8,128]{3,2,1,0:T(8,128)S(1)} %get-tuple-element.4) | data formatting | bytes 196608
  20.5 0.7 %copy.9 = f32[64,512]{1,0:T(8,128)} copy(f32[64,512]{1,0:T(8,128)S(1)} %get-tuple-element.5) | data formatting | bytes 262144

commit v6 on v4

--- a/solution.py
+++ b/solution.py
@@ -21,7 +21,10 @@
 
 MESH = pl.DeviceIdType.MESH
 SIGNS = (-1, 0, 1)
-OFFSETS = [(a, b, c) for a in SIGNS for b in SIGNS for c in SIGNS if (a, b, c) != (0, 0, 0)]
+OFFSETS = sorted(
+    [(a, b, c) for a in SIGNS for b in SIGNS for c in SIGNS if (a, b, c) != (0, 0, 0)],
+    key=lambda o: (abs(o[0]) + abs(o[1]) + abs(o[2]), abs(o[2])),
+)
 
 
 def side(sign):
@@ -76,6 +79,7 @@
     from_cols,
     ext,
     image,
+    spreader,
     height,
     conduct,
     work,
@@ -132,7 +136,7 @@
     conduct[krow : krow + rows, width + cols :] = jnp.zeros((rows, width), conduct.dtype)
 
     barrier = pltpu.get_barrier_semaphore()
-    for a, b, c in reversed(others):
+    for a, b, c in others:
         pl.semaphore_signal(barrier, inc=1, device_id=(xs[a], ys[b], zs[c]), device_id_type=MESH)
 
     ratio_r, ratio_c = rows // cells, cols // width
@@ -241,6 +245,28 @@
 
     for o in surf_offsets:
         pl.when(surf_present(*o, False))(lambda o=o: surf_start(*o))
+
+    tall, span = rows + 2 * STEPS, share + width
+    row_at = x * rows - STEPS + lax.broadcasted_iota(jnp.int32, (tall, span), 0)
+    lane_at = lax.broadcasted_iota(jnp.int32, (tall, span), 1)
+    lane_at = jnp.where(lane_at >= span - width // 2, lane_at - span, lane_at)
+    col_at = y * cols + z * share + lane_at
+    inside[...] = jnp.where(
+        (row_at >= 0) & (row_at < rows * nx) & (col_at >= 0) & (col_at < cols * ny), time_step, 0.0
+    )
+
+    cell_at = lax.broadcasted_iota(jnp.int32, (width, share), 0) * ratio_c
+    col = z * share + lax.broadcasted_iota(jnp.int32, (width, share), 1)
+    spreader[...] = jnp.where((col >= cell_at) & (col < cell_at + ratio_c), 1.0, 0.0).astype(jnp.bfloat16)
+    for o in OFFSETS:
+        pl.when(present(*o))(lambda o=o: rim_copy(*o).wait_send())
+    for b, c in surf_offsets:
+
+        def sent(b=b, c=c):
+            for copy in surf_copies(b, c):
+                copy.wait_send()
+
+        pl.when(surf_present(b, c, False))(sent)
 
     for a, b, c in OFFSETS:
         pl.when(present(a, b, c))(lambda o=(-a, -b, -c): rim_copy(*o).wait_recv())
@@ -349,7 +375,6 @@
         pl.when(surf_present(b, c, True))(arrived)
     loads[3].wait()
     start = pl.multiple_of(z * share, share)
-    tall = rows + 2 * STEPS
     left_half = lax.broadcasted_iota(jnp.int32, (1, width), 1) < width // 2
 
     def joined_window(ref):
@@ -359,48 +384,33 @@
 
     work[...] = joined_window(height)
     k = joined_window(conduct)[krow - STEPS : krow + rows + STEPS]
-    span = share + width
     face_right[...] = 0.5 * (k + pltpu.roll(k, span - 1, 1))
     face_down[...] = 0.5 * (k + pltpu.roll(k, tall - 1, 0))
-    row_at = x * rows - STEPS + lax.broadcasted_iota(jnp.int32, (tall, span), 0)
-    lane_at = lax.broadcasted_iota(jnp.int32, (tall, span), 1)
-    lane_at = jnp.where(lane_at >= span - width // 2, lane_at - span, lane_at)
-    col_at = y * cols + z * share + lane_at
-    inside[...] = jnp.where(
-        (row_at >= 0) & (row_at < rows * nx) & (col_at >= 0) & (col_at < cols * ny), time_step, 0.0
-    )
-
-    def diffuse(_, carry):
+    def stepped():
         h = work[...]
         s = pltpu.roll(h, span - 1, 1) - h
         along = face_right[...] * s * lax.rsqrt(1.0 + s * s)
         s = pltpu.roll(h, tall - 1, 0) - h
         across = face_down[...] * s * lax.rsqrt(1.0 + s * s)
         change = along - pltpu.roll(along, 1, 1) + across - pltpu.roll(across, 1, 0)
-        work[...] = h + inside[...] * change
+        return h + inside[...] * change
+
+    def diffuse(_, carry):
+        for _ in range(2):
+            work[...] = stepped()
         return carry
 
-    lax.fori_loop(0, STEPS, diffuse, 0)
+    lax.fori_loop(0, (STEPS - 1) // 2, diffuse, 0)
+    for _ in range((STEPS - 1) % 2):
+        work[...] = stepped()
+    surface_ref[...] = stepped()[STEPS : STEPS + rows, 0:share]
 
     @pl.when(jnp.logical_not(is_top))
     def _():
         top_copy(1).wait_recv()
         top_own[...] = top_in[...]
 
-    cell_at = lax.broadcasted_iota(jnp.int32, (width, share), 0) * ratio_c
-    col = z * share + lax.broadcasted_iota(jnp.int32, (width, share), 1)
-    pick = jnp.where((col >= cell_at) & (col < cell_at + ratio_c), 1.0, 0.0)
-    spread = picked(top_own[...].reshape(2 * cells, width), pick.astype(jnp.bfloat16))
-
-    for o in OFFSETS:
-        pl.when(present(*o))(lambda o=o: rim_copy(*o).wait_send())
-    for b, c in surf_offsets:
-
-        def sent(b=b, c=c):
-            for copy in surf_copies(b, c):
-                copy.wait_send()
-
-        pl.when(surf_present(b, c, False))(sent)
+    spread = picked(top_own[...].reshape(2 * cells, width), spreader[...])
 
     @pl.when(is_top)
     def _():
@@ -428,7 +438,7 @@
         velocity_ref[f] = on_b * field[f] + on_ab * image[f, 1:-1, 0:cells, 0:width]
     rise = (STEPS * time_step) * (on_b * spread[:cells] + on_ab * spread[cells:])
     rise = jnp.broadcast_to(rise[:, None, :], (cells, ratio_r, share)).reshape(rows, share)
-    surface_ref[...] = work[STEPS : STEPS + rows, 0:share] + rise
+    surface_ref[...] = surface_ref[...] + rise
 
 
 def local(sizes, body_force, viscosity, topography, kappa):
@@ -457,6 +467,7 @@
             pltpu.VMEM((9, 2, cells, width), f32),
             pltpu.VMEM((4, depth + 2 * REACH, 2 * cells, 2 * width), f32),
             pltpu.VMEM((3, depth + 2 * REACH - 2, 2 * cells, 2 * width), f32),
+            pltpu.VMEM((width, share), jnp.bfloat16),
             pltpu.VMEM((rows + 2 * STEPS, cols + 2 * width), f32),
             pltpu.VMEM((rows + 32, cols + 2 * width), kappa.dtype),
             pltpu.VMEM((rows + 2 * STEPS, share + width), f32),

time: 19.3 us -> 19.2 us (level)
  no operation moved by 1% of the time
where the time goes in v6:
time: 19.2 us; the launch traced here: 19 us
  Pallas kernels  17.1 us (89%)
  local copies, waits for them, and re-layouts  1.3 us (7%)
  between operations  0.64 us (3%)
    pallas_call x1, Pallas kernels, local(): pl.pallas_call(functools.partial(kernel, sizes), out_shape=(jax.ShapeDtyp...  17.1 us
    unnamed x2, local copies, waits for them, and re-layouts  1.3 us

profile of v6, /device:TPU:0, one launch (start us, length us, event | category | flops | bytes accessed | tf_op | source)
XLA Modules:
  0.0 19.0 jit_solution(2571771211477348440)
XLA Ops:
  0.6 17.1 %shard_map.59 = (f32[3,8,8,128]{3,2,1,0:T(8,128)S(1)}, f32[64,512]{1,0:T(8,128)S(1)}) custom-call(f32[3,8,8,128]{3,2,1,0:T(8,128)} %force_hbm.1, f32[8,8,128]{2,1,0:T(8,128)} %visc_hbm.1, f32[64,1024]{1,0:T(8,128)} %topo_hbm.1, bf16[64,1024]{1,0:T(8,128)(2,1)} %kappa_hbm.1), custom_call_target="tpu_custom_call" | custom-call | tf_op jit(solution)/shard_map/pallas_call | solution.py:452
  17.7 0.6 %copy.8 = f32[3,8,8,128]{3,2,1,0:T(8,128)} copy(f32[3,8,8,128]{3,2,1,0:T(8,128)S(1)} %get-tuple-element.4) | data formatting | bytes 196608
  18.4 0.7 %copy.9 = f32[64,512]{1,0:T(8,128)} copy(f32[64,512]{1,0:T(8,128)S(1)} %get-tuple-element.5) | data formatting | bytes 262144

commit v7 on v6

--- a/solution.py
+++ b/solution.py
@@ -35,14 +35,18 @@
     return (a + 1) * 9 + (b + 1) * 3 + (c + 1)
 
 
-def weighted(u):
-    rows, lanes = u.shape[1:]
-    beside = pltpu.roll(u, 1, 2) + pltpu.roll(u, lanes - 1, 2)
-    near = W_FACE * u + W_EDGE * beside
-    far = W_EDGE * u + W_CORNER * beside
-    level = W_FACE * beside[1:-1] + (near[:-2] + near[2:])
-    next_row = near[1:-1] + (far[:-2] + far[2:])
-    return level + (pltpu.roll(next_row, 1, 1) + pltpu.roll(next_row, rows - 1, 1))
+def weighted(layers):
+    held = []
+    for u in layers:
+        rows, lanes = u.shape
+        beside = pltpu.roll(u, 1, 1) + pltpu.roll(u, lanes - 1, 1)
+        held.append((W_FACE * beside, W_FACE * u + W_EDGE * beside, W_EDGE * u + W_CORNER * beside))
+        if len(held) == 3:
+            (_, near0, far0), (level, near1, _), (_, near2, far2) = held
+            level = level + (near0 + near2)
+            next_row = near1 + (far0 + far2)
+            yield level + (pltpu.roll(next_row, 1, 0) + pltpu.roll(next_row, rows - 1, 0))
+            held.pop(0)
 
 
 def picked(x, choice):
@@ -58,7 +62,6 @@
 
 
 def total(x):
-    x = x.reshape((-1,) + x.shape[-2:]).sum(axis=0)
     return x.sum(axis=(0, 1), keepdims=True)
 
 
@@ -79,6 +82,8 @@
     from_cols,
     ext,
     image,
+    gain,
+    again,
     spreader,
     height,
     conduct,
@@ -152,32 +157,40 @@
                 yes = one if yes is None else jnp.logical_and(yes, one)
         return yes
 
+    loads[1].wait()
+    loads[2].wait()
+    lane = lax.broadcasted_iota(jnp.int32, (cells, width), 1)
+    sub = lax.broadcasted_iota(jnp.int32, (cells, width), 0)
+
+    def in_lane_pack(f, d, tile, packed):
+        j = f * depth + d
+        return jnp.where((lane >= 4 * j) & (lane < 4 * j + 4), pltpu.roll(tile, (4 * j + 2) % width, 1), packed)
+
+    def in_row_pack(f, d, tile, packed, first_row):
+        p = (d % 2) * 2 + f % 2
+        turn = (2 * p - first_row) % cells
+        return jnp.where((sub >= 2 * p) & (sub < 2 * p + 2), pltpu.roll(tile, turn, 0) if turn else tile, packed)
+
+    packed = jnp.zeros((cells, width), jnp.float32)
+    for f in range(4):
+        for d in range(depth):
+            packed = in_lane_pack(f, d, field[f, d], packed)
+    for t in range(depth):
+        for i, first_row in enumerate((0, cells - 2)):
+            rim = jnp.zeros((cells, width), jnp.float32)
+            for d in (t // 2 * 2, t // 2 * 2 + 1):
+                for f in (t % 2 * 2, t % 2 * 2 + 1):
+                    rim = in_row_pack(f, d, field[f, d], rim, first_row)
+            row_pack[i, t] = rim
+
     loads[0].wait()
     by_rows = height[STEPS : STEPS + rows, width : width + cols].reshape(cells, ratio_r, cols).sum(axis=1)
     load = picked(by_rows, pick) * (1.0 / (ratio_r * ratio_c))
-    loads[1].wait()
-    loads[2].wait()
-    field[2, depth - 1] = field[2, depth - 1] + jnp.where(is_top, -load_gain * load, 0.0)
-
-    lane = lax.broadcasted_iota(jnp.int32, (cells, width), 1)
-    sub = lax.broadcasted_iota(jnp.int32, (cells, width), 0)
-    packed = jnp.zeros((cells, width), jnp.float32)
-    up_pack, down_pack = {}, {}
-    for f in range(4):
-        for d in range(depth):
-            tile = field[f, d]
-            j = f * depth + d
-            packed = jnp.where((lane >= 4 * j) & (lane < 4 * j + 4), pltpu.roll(tile, (4 * j + 2) % width, 1), packed)
-            t, p = (d // 2) * 2 + f // 2, (d % 2) * 2 + f % 2
-            chosen = (sub >= 2 * p) & (sub < 2 * p + 2)
-            up = pltpu.roll(tile, (2 * p) % 8, 0) if p else tile
-            down = pltpu.roll(tile, (2 * p + 2) % 8, 0) if (2 * p + 2) % 8 else tile
-            up_pack[t] = jnp.where(chosen, up, up_pack.get(t, 0.0))
-            down_pack[t] = jnp.where(chosen, down, down_pack.get(t, 0.0))
-    lane_pack[...] = packed
-    for t in range(depth):
-        row_pack[0, t] = up_pack[t]
-        row_pack[1, t] = down_pack[t]
+    loaded = field[2, depth - 1] + jnp.where(is_top, -load_gain * load, 0.0)
+    field[2, depth - 1] = loaded
+    lane_pack[...] = in_lane_pack(2, depth - 1, loaded, packed)
+    for i, first_row in enumerate((0, cells - 2)):
+        row_pack[i, depth - 1] = in_row_pack(2, depth - 1, loaded, row_pack[i, depth - 1], first_row)
 
     def rim_copy(a, b, c):
         span = slice(depth - 2, depth) if a > 0 else slice(0, 2)
@@ -301,36 +314,37 @@
                     tile = pltpu.roll(joined[r], turn, 1) if turn else joined[r]
                     ext[f, layer, r * cells : (r + 1) * cells, width:] = tile
 
-    eta = ext[3]
-    gain = drag + W_ALL * eta[1:-1] + weighted(eta)
-    for f in range(3):
-        v = ext[f]
-        out = gain * v[1:-1] - eta[1:-1] * weighted(v) - weighted(eta * v)
-        image[f] = jnp.where(eta[1:-1] > 0.0, out, 0.0)
-    eta1 = eta[1:-1]
-    center = (slice(None), slice(0, cells), slice(0, width))
+    wide = depth + 2 * REACH
+    for d, k in enumerate(weighted(ext[3, d] for d in range(wide))):
+        gain[d] = drag + W_ALL * ext[3, d + 1] + k
     m0 = m1 = jnp.zeros((cells, width), jnp.float32)
     for f in range(3):
-        b = field[f]
-        ab = image[f, 1:-1, 0:cells, 0:width]
-        m0 = m0 + (b * b).sum(axis=0)
-        m1 = m1 + (b * ab).sum(axis=0)
+        for d, k in enumerate(weighted(ext[f, d] for d in range(wide))):
+            image[f, d] = gain[d] * ext[f, d + 1] - ext[3, d + 1] * k
+        for d, k in enumerate(weighted(ext[3, d] * ext[f, d] for d in range(wide))):
+            out = jnp.where(ext[3, d + 1] > 0.0, image[f, d] - k, 0.0)
+            image[f, d] = out
+            if 0 < d <= depth:
+                b = field[f, d - 1]
+                m0 = m0 + b * b
+                m1 = m1 + b * out[0:cells, 0:width]
     m0, m1 = total(m0), total(m1)
     own = jnp.where(m0 > 0.0, m1 / m0, 0.0)
+    for f in range(3):
+        for d, k in enumerate(weighted(image[f, d] for d in range(wide - 2))):
+            ab = image[f, d + 1, 0:cells, 0:width]
+            again[f, d] = gain[d + 1, 0:cells, 0:width] * ab - field[3, d] * k[0:cells, 0:width]
+        for d, k in enumerate(weighted(ext[3, d + 1] * image[f, d] for d in range(wide - 2))):
+            again[f, d] = again[f, d] - k[0:cells, 0:width]
     sums = [jnp.zeros((cells, width), jnp.float32) for _ in range(4)]
     for f in range(3):
-        v = image[f]
-        b = field[f]
-        ab = v[1:-1][center]
-        again = (
-            gain[1:-1][center] * ab
-            - eta1[1:-1][center] * weighted(v)[center]
-            - weighted(eta1 * v)[center]
-        )
-        w = ab - own * b
-        aw = again - own * ab
-        for i, (p, q) in enumerate(((w, b), (w, w), (w, aw), (b, aw))):
-            sums[i] = sums[i] + (p * q).sum(axis=0)
+        for d in range(depth):
+            b = field[f, d]
+            ab = image[f, d + 1, 0:cells, 0:width]
+            w = ab - own * b
+            aw = again[f, d] - own * ab
+            for i, (p, q) in enumerate(((w, b), (w, w), (w, aw), (b, aw))):
+                sums[i] = sums[i] + p * q
     numbers = [m0, m1, own] + [total(s) for s in sums]
     spot = lax.broadcasted_iota(jnp.int32, (1, width), 1)
     line = jnp.zeros((1, width), jnp.float32)
@@ -467,6 +481,8 @@
             pltpu.VMEM((9, 2, cells, width), f32),
             pltpu.VMEM((4, depth + 2 * REACH, 2 * cells, 2 * width), f32),
             pltpu.VMEM((3, depth + 2 * REACH - 2, 2 * cells, 2 * width), f32),
+            pltpu.VMEM((depth + 2 * REACH - 2, 2 * cells, 2 * width), f32),
+            pltpu.VMEM((3, depth, cells, width), f32),
             pltpu.VMEM((width, share), jnp.bfloat16),
             pltpu.VMEM((rows + 2 * STEPS, cols + 2 * width), f32),
             pltpu.VMEM((rows + 32, cols + 2 * width), kappa.dtype),

time: 19.2 us -> 19 us (0.990)
  Pallas kernels: 17.1 us -> 16.9 us
where the time goes in v7:
time: 19 us; the launch traced here: 18.9 us
  Pallas kernels  16.9 us (89%)
  local copies, waits for them, and re-layouts  1.3 us (7%)
  between operations  0.64 us (3%)
    pallas_call x1, Pallas kernels, local(): pl.pallas_call(functools.partial(kernel, sizes), out_shape=(jax.ShapeDtyp...  16.9 us
    unnamed x2, local copies, waits for them, and re-layouts  1.3 us

profile of v7, /device:TPU:0, one launch (start us, length us, event | category | flops | bytes accessed | tf_op | source)
XLA Modules:
  0.0 18.9 jit_solution(16601843462754484010)
XLA Ops:
  0.6 16.9 %shard_map.59 = (f32[3,8,8,128]{3,2,1,0:T(8,128)S(1)}, f32[64,512]{1,0:T(8,128)S(1)}) custom-call(f32[3,8,8,128]{3,2,1,0:T(8,128)} %force_hbm.1, f32[8,8,128]{2,1,0:T(8,128)} %visc_hbm.1, f32[64,1024]{1,0:T(8,128)} %topo_hbm.1, bf16[64,1024]{1,0:T(8,128)(2,1)} %kappa_hbm.1), custom_call_target="tpu_custom_call" | custom-call | tf_op jit(solution)/shard_map/pallas_call | solution.py:466
  17.6 0.6 %copy.8 = f32[3,8,8,128]{3,2,1,0:T(8,128)} copy(f32[3,8,8,128]{3,2,1,0:T(8,128)S(1)} %get-tuple-element.4) | data formatting | bytes 196608
  18.2 0.7 %copy.9 = f32[64,512]{1,0:T(8,128)} copy(f32[64,512]{1,0:T(8,128)S(1)} %get-tuple-element.5) | data formatting | bytes 262144

commit v8 on v7

--- a/solution.py
+++ b/solution.py
@@ -33,6 +33,18 @@
 
 def code(a, b, c):
     return (a + 1) * 9 + (b + 1) * 3 + (c + 1)
+
+
+def partner(at, k, size):
+    if size & (size - 1):
+        return lax.rem(at + k, size)
+    bit = 1
+    moved = at
+    while bit < size:
+        if k & bit:
+            moved = moved + bit * (1 - 2 * lax.rem(lax.div(at, bit), 2))
+        bit *= 2
+    return moved
 
 
 def weighted(layers):
@@ -113,11 +125,11 @@
     share = cols // nz
     krow = 16
 
-    xs = [lax.rem(x + k, nx) for k in range(nx)]
-    ys = [lax.rem(y + k, ny) for k in range(ny)]
-    zs = [lax.rem(z + k, nz) for k in range(nz)]
+    xs = [partner(x, k, nx) for k in range(nx)]
+    ys = [partner(y, k, ny) for k in range(ny)]
+    zs = [partner(z, k, nz) for k in range(nz)]
     others = [(a, b, c) for a in range(nx) for b in range(ny) for c in range(nz)][1:]
-    others.sort(key=lambda o: -(min(o[0], nx - o[0]) + min(o[1], ny - o[1]) + min(o[2], nz - o[2])))
+    others.sort(key=lambda o: -(o[0] // 2 + o[1] + o[2]))
     is_top = z == nz - 1
 
     loads = [
@@ -141,7 +153,7 @@
     conduct[krow : krow + rows, width + cols :] = jnp.zeros((rows, width), conduct.dtype)
 
     barrier = pltpu.get_barrier_semaphore()
-    for a, b, c in others:
+    for a, b, c in reversed(others):
         pl.semaphore_signal(barrier, inc=1, device_id=(xs[a], ys[b], zs[c]), device_id_type=MESH)
 
     ratio_r, ratio_c = rows // cells, cols // width

time: 19 us -> 19.2 us (1.011)
  Pallas kernels: 16.9 us -> 17.1 us
where the time goes in v8:
time: 19.2 us; the launch traced here: 19 us
  Pallas kernels  17.1 us (89%)
  local copies, waits for them, and re-layouts  1.3 us (7%)
  between operations  0.64 us (3%)
    pallas_call x1, Pallas kernels, local(): pl.pallas_call(functools.partial(kernel, sizes), out_shape=(jax.ShapeDtyp...  17.1 us
    unnamed x2, local copies, waits for them, and re-layouts  1.3 us

profile of v8, /device:TPU:0, one launch (start us, length us, event | category | flops | bytes accessed | tf_op | source)
XLA Modules:
  0.0 19.0 jit_solution(17550756668133453136)
XLA Ops:
  0.6 17.1 %shard_map.59 = (f32[3,8,8,128]{3,2,1,0:T(8,128)S(1)}, f32[64,512]{1,0:T(8,128)S(1)}) custom-call(f32[3,8,8,128]{3,2,1,0:T(8,128)} %force_hbm.1, f32[8,8,128]{2,1,0:T(8,128)} %visc_hbm.1, f32[64,1024]{1,0:T(8,128)} %topo_hbm.1, bf16[64,1024]{1,0:T(8,128)(2,1)} %kappa_hbm.1), custom_call_target="tpu_custom_call" | custom-call | tf_op jit(solution)/shard_map/pallas_call | solution.py:478
  17.7 0.6 %copy.8 = f32[3,8,8,128]{3,2,1,0:T(8,128)} copy(f32[3,8,8,128]{3,2,1,0:T(8,128)S(1)} %get-tuple-element.4) | data formatting | bytes 196608
  18.4 0.7 %copy.9 = f32[64,512]{1,0:T(8,128)} copy(f32[64,512]{1,0:T(8,128)S(1)} %get-tuple-element.5) | data formatting | bytes 262144
